TPU v7x, 32 devices: a whole 2x2x4 slice. The times are simulated.
32 devices in a mesh: dp: 4 (over z), expert: 8 (over y, x, core).
Axes of the slice: x: 2, y: 2, z: 4, core: 2. Of those that a mesh axis runs over, the one named last changes fastest.
Arguments:
- tokens: bfloat16 [512, 4096], P(('dp', 'expert')), may hold values from -6 to 6
- units: int32 [512, 8], P(('dp', 'expert')), may hold values from 0 to 23, as said below
- replicas: int32 [8], replicated, may hold values from 0 to 15, as said below
- route_probs: float32 [512, 8], P(('dp', 'expert')), may hold values from 0.05 to 1
- cotangent: bfloat16 [512, 4096], P(('dp', 'expert')), may hold values from -4 to 4
- w_gate: bfloat16 [16, 4096, 768], P('expert', 'dp'), may hold values from -0.09375 to 0.09375
- w_up: bfloat16 [16, 4096, 768], P('expert', 'dp'), may hold values from -0.09375 to 0.09375
- w_down: bfloat16 [16, 768, 4096], P('expert', None, 'dp'), may hold values from -0.21875 to 0.21875
Outputs:
- layer_out: bfloat16 [512, 4096], P(('dp', 'expert'))
- d_tokens: bfloat16 [512, 4096], P(('dp', 'expert'))
- d_probs: float32 [512, 8], P(('dp', 'expert'))
- d_gate_w: bfloat16 [16, 4096, 768], P('expert', 'dp')
- d_up_w: bfloat16 [16, 4096, 768], P('expert', 'dp')
- d_down_w: bfloat16 [16, 768, 4096], P('expert', None, 'dp')
Inputs may be any that keep to these rules, and one draw needn't show every extreme that they name: `replicas`: the copy on index o of expert serves one of the 2 experts homed on index (o + 8 - 8 // 2) % 8. `units`: each token's 8 rows name 8 different copies of 8 different experts. Within the rows of one device (aligned blocks of 16 tokens) no copy is named more than 6 times, and in every block some copy is named exactly 6 times.
All inputs are finite; a program needn't handle non-finite values.
Results may differ from a plain program's by a relative error of at most 0.029.
Values may be sent and summed in bfloat16 or wider, within the bound.
A program may use at most 128 MiB of HBM per device.

v0:
```python
import jax
import jax.numpy as jnp
from jax import lax
from jax.sharding import PartitionSpec as P


def passed_along(array, axis, by):
    length = lax.axis_size(axis)
    return lax.ppermute(array, axis, [(i, (i + by) % length) for i in range(length)])


def activate(gate_sum, up_sum):
    return (gate_sum * jax.nn.sigmoid(gate_sum) * up_sum).astype(jnp.bfloat16)


def derive(gate_sum, up_sum, grad_hidden):
    sigmoid_gate = jax.nn.sigmoid(gate_sum)
    silu_gate = gate_sum * sigmoid_gate
    grad_gate = (
        grad_hidden * up_sum * sigmoid_gate * (1.0 + gate_sum * (1.0 - sigmoid_gate))
    ).astype(jnp.bfloat16)
    grad_up = (grad_hidden * silu_gate).astype(jnp.bfloat16)
    return (grad_gate, grad_up)


def local(tokens, units, replicas, route_probs, cotangent, w_gate, w_up, w_down):
    groups = lax.axis_size("dp")
    owners = lax.axis_size("expert")
    per_owner = w_gate.shape[0]
    per_unit = per_owner + 1
    unit_total = per_unit * owners
    hidden_units = w_gate.shape[2]
    token_count = units.shape[0]
    top_count = units.shape[1]
    model_width = tokens.shape[1]
    row_total = token_count * top_count
    capacity = (row_total + unit_total - 1) // unit_total
    half = owners // 2
    my_index = lax.axis_index("expert")
    lent = replicas[(my_index + half) % owners] - my_index * per_owner
    lent_gate = lax.dynamic_index_in_dim(w_gate, lent, 0, keepdims=False)
    lent_up = lax.dynamic_index_in_dim(w_up, lent, 0, keepdims=False)
    lent_down = lax.dynamic_index_in_dim(w_down, lent, 0, keepdims=False)
    extra_gate, extra_up, extra_down = passed_along((lent_gate, lent_up, lent_down), "expert", half)
    flat_units = units.reshape(-1)
    onehot = (flat_units[:, None] == jnp.arange(unit_total, dtype=jnp.int32)[None, :]).astype(
        jnp.int32
    )
    rank_rows = jnp.sum(onehot * (jnp.cumsum(onehot, axis=0) - 1), axis=1)
    where_to = flat_units * capacity + rank_rows
    select = (
        where_to[None, :] == jnp.arange(unit_total * capacity, dtype=jnp.int32)[:, None]
    ).astype(jnp.bfloat16)
    token_rows = jnp.repeat(tokens, top_count, axis=0)
    flat_probs = route_probs.reshape(-1)
    scaled_rows = (
        flat_probs[:, None] * jnp.repeat(cotangent, top_count, axis=0).astype(jnp.float32)
    ).astype(jnp.bfloat16)
    send_rows = jnp.dot(select, token_rows, preferred_element_type=jnp.float32).astype(jnp.bfloat16)
    send_scaled = jnp.dot(select, scaled_rows, preferred_element_type=jnp.float32).astype(
        jnp.bfloat16
    )
    send_rows = send_rows.reshape(owners, per_unit, capacity, model_width)
    send_scaled = send_scaled.reshape(owners, per_unit, capacity, model_width)
    recv_rows, recv_scaled = (
        lax.all_to_all(
            lax.all_to_all(send_rows, "dp", split_axis=3, concat_axis=2, tiled=True),
            "expert",
            split_axis=0,
            concat_axis=0,
            tiled=True,
        ),
        lax.all_to_all(
            lax.all_to_all(send_scaled, "dp", split_axis=3, concat_axis=2, tiled=True),
            "expert",
            split_axis=0,
            concat_axis=0,
            tiled=True,
        ),
    )
    slot_block = groups * capacity
    slot_total = owners * slot_block
    gate_units = jnp.concatenate([w_gate, extra_gate[None]], axis=0)
    up_units = jnp.concatenate([w_up, extra_up[None]], axis=0)
    down_units = jnp.concatenate([w_down, extra_down[None]], axis=0)
    partial_gate = jnp.einsum(
        "cusd,udf->ucsf", recv_rows, gate_units, preferred_element_type=jnp.float32
    )
    partial_up = jnp.einsum(
        "cusd,udf->ucsf", recv_rows, up_units, preferred_element_type=jnp.float32
    )
    partial_gate = partial_gate.reshape(per_unit, slot_total, hidden_units)
    partial_up = partial_up.reshape(per_unit, slot_total, hidden_units)
    gate_sum, up_sum = (
        lax.psum(partial_gate.astype(jnp.bfloat16), "dp").astype(jnp.float32),
        lax.psum(partial_up.astype(jnp.bfloat16), "dp").astype(jnp.float32),
    )
    hidden = activate(gate_sum, up_sum)
    hidden_four = hidden.reshape(per_unit, owners, slot_block, hidden_units)
    expert_out = jnp.einsum(
        "ucsf,ufd->cusd", hidden_four, down_units, preferred_element_type=jnp.float32
    ).astype(jnp.bfloat16)
    returned = lax.all_to_all(
        lax.all_to_all(expert_out, "dp", split_axis=2, concat_axis=3, tiled=True),
        "expert",
        split_axis=0,
        concat_axis=0,
        tiled=True,
    )
    row_out = jnp.dot(
        select.T,
        returned.reshape(unit_total * capacity, model_width),
        preferred_element_type=jnp.float32,
    )
    row_out = row_out.reshape(token_count, top_count, model_width)
    layer_out = jnp.sum(route_probs[:, :, None] * row_out, axis=1).astype(jnp.bfloat16)
    d_probs = jnp.sum(row_out * cotangent.astype(jnp.float32)[:, None, :], axis=2)
    partial_grad = jnp.einsum(
        "cusd,ufd->ucsf", recv_scaled, down_units, preferred_element_type=jnp.float32
    )
    partial_grad = partial_grad.reshape(per_unit, slot_total, hidden_units)
    grad_hidden = lax.psum(partial_grad.astype(jnp.bfloat16), "dp").astype(jnp.float32)
    grad_gate, grad_up = derive(gate_sum, up_sum, grad_hidden)
    gate_four = grad_gate.reshape(per_unit, owners, slot_block, hidden_units)
    up_four = grad_up.reshape(per_unit, owners, slot_block, hidden_units)
    down_copies = jnp.einsum(
        "ucsf,cusd->ufd", hidden_four, recv_scaled, preferred_element_type=jnp.float32
    )
    gate_copies = jnp.einsum(
        "cusd,ucsf->udf", recv_rows, gate_four, preferred_element_type=jnp.float32
    )
    up_copies = jnp.einsum("cusd,ucsf->udf", recv_rows, up_four, preferred_element_type=jnp.float32)
    back_gate, back_up, back_down = passed_along(
        (
            gate_copies[per_owner].astype(jnp.bfloat16),
            up_copies[per_owner].astype(jnp.bfloat16),
            down_copies[per_owner].astype(jnp.bfloat16),
        ),
        "expert",
        owners - half,
    )
    marked = (jnp.arange(per_owner, dtype=jnp.int32) == lent).astype(jnp.float32)[:, None, None]
    d_gate_w = (gate_copies[:per_owner] + marked * back_gate.astype(jnp.float32)[None]).astype(
        jnp.bfloat16
    )
    d_up_w = (up_copies[:per_owner] + marked * back_up.astype(jnp.float32)[None]).astype(
        jnp.bfloat16
    )
    d_down_w = (down_copies[:per_owner] + marked * back_down.astype(jnp.float32)[None]).astype(
        jnp.bfloat16
    )
    expert_grad = (
        jnp.einsum("ucsf,udf->cusd", gate_four, gate_units, preferred_element_type=jnp.float32)
        + jnp.einsum("ucsf,udf->cusd", up_four, up_units, preferred_element_type=jnp.float32)
    ).astype(jnp.bfloat16)
    grad_back = lax.all_to_all(
        lax.all_to_all(expert_grad, "dp", split_axis=2, concat_axis=3, tiled=True),
        "expert",
        split_axis=0,
        concat_axis=0,
        tiled=True,
    )
    row_grad = jnp.dot(
        select.T,
        grad_back.reshape(unit_total * capacity, model_width),
        preferred_element_type=jnp.float32,
    )
    d_tokens = jnp.sum(row_grad.reshape(token_count, top_count, model_width), axis=1).astype(
        jnp.bfloat16
    )
    return (layer_out, d_tokens, d_probs, d_gate_w, d_up_w, d_down_w)


def solution(mesh):
    return jax.shard_map(
        local,
        mesh=mesh,
        in_specs=(
            P(("dp", "expert"), None),
            P(("dp", "expert"), None),
            P(),
            P(("dp", "expert"), None),
            P(("dp", "expert"), None),
            P("expert", "dp", None),
            P("expert", "dp", None),
            P("expert", None, "dp"),
        ),
        out_specs=(
            P(("dp", "expert"), None),
            P(("dp", "expert"), None),
            P(("dp", "expert"), None),
            P("expert", "dp", None),
            P("expert", "dp", None),
            P("expert", None, "dp"),
        ),
        check_vma=False,
    )
```

profile of v0, /device:TPU:0, one launch (start us, length us, event | category | flops | bytes accessed | tf_op | source)
XLA Modules:
  0.0 734.4 jit_solution(4978336262759930776)
XLA Ops:
  9.4 21.4 %copy.93 = bf16[8,3,6,4096]{2,0,1,3:T(8,128)(2,1)} copy(bf16[8,3,6,4096]{3,2,1,0:T(8,128)(2,1)S(1)} %reshape.97) | data formatting | bytes 2359296 | tf_op jit(solution)/shard_map/reshape | solution.py:63
  30.8 69.4 %reshape.116 = bf16[4,2,73728]{2,1,0:T(2,128)(2,1)} reshape(bf16[4096,3,8,6]{3,2,1,0:T(8,128)(2,1)} %bitcast.103) | data formatting | bytes 2359296
  100.2 6.5 all-to-all-start
  109.9 21.4 %copy.104 = bf16[8,3,6,4096]{2,0,1,3:T(8,128)(2,1)} copy(bf16[8,3,6,4096]{3,2,1,0:T(8,128)(2,1)S(1)} %reshape.100) | data formatting | bytes 2359296 | tf_op jit(solution)/shard_map/reshape | solution.py:64
  131.2 69.9 %reshape.118 = bf16[4,2,73728]{2,1,0:T(2,128)(2,1)} reshape(bf16[4096,3,8,6]{3,2,1,0:T(8,128)(2,1)} %bitcast.104) | data formatting | bytes 2359296
  201.1 5.1 all-to-all-start.4
  207.5 2.7 dynamic-slice_bitcast_fusion
  211.6 69.3 %reshape.117 = bf16[4096,3,8,6]{3,2,1,0:T(8,128)(2,1)} reshape(bf16[4,2,73728]{2,1,0:T(2,128)(2,1)S(1)} %all-to-all-done) | data formatting | bytes 2359296
  280.9 25.8 %copy.121 = bf16[8,3,6,4,1024]{4,3,0,2,1:T(4,128)(2,1)S(1)} copy(bf16[8,3,6,4,1024]{2,0,1,4,3:T(8,128)(2,1)} %bitcast.105) | data formatting | bytes 2359296 | tf_op jit(solution)/shard_map/all_to_all | solution.py:67
  308.8 4.5 all-to-all-start.1
  314.9 2.0 collective-permute-start.1
  318.9 69.3 %reshape.119 = bf16[4096,3,8,6]{3,2,1,0:T(8,128)(2,1)} reshape(bf16[4,2,73728]{2,1,0:T(2,128)(2,1)S(1)} %all-to-all-done.4) | data formatting | bytes 2359296
  388.1 25.8 %copy.124 = bf16[8,3,6,4,1024]{4,3,0,2,1:T(4,128)(2,1)S(1)} copy(bf16[8,3,6,4,1024]{2,0,1,4,3:T(8,128)(2,1)} %bitcast.106) | data formatting | bytes 2359296 | tf_op jit(solution)/shard_map/all_to_all | solution.py:74
  416.0 3.6 all-to-all-start.5
  420.1 5.0 fusion.25
  425.1 3.8 fusion.24
  428.9 7.5 %all-to-all-done.5 = bf16[8,3,24,1024]{3,2,1,0:T(8,128)(2,1)S(1)} async-done(((bf16[8,3,24,1024]{3,2,1,0:T(8,128)(2,1)}), bf16[8,3,24,1024]{3,2,1,0:T(8,128)(2,1)S(1)}, u32[]{:S(2)}, u32[]{:S(2)}) %all-to-all-start.5) | async-done | bytes 1179680 | tf_op jit(solution)/shard_map/all_to_all | solution.py:73
  436.4 5.4 fusion.23
  441.9 105.6 %all-reduce.3.cloned.1.call-done = (bf16[3,192,768]{2,1,0:T(8,128)(2,1)}, bf16[3,192,768]{2,1,0:T(8,128)(2,1)}, bf16[3,192,768]{2,1,0:T(8,128)(2,1)}) async-done(((bf16[3,192,768]{2,1,0:T(8,128)(2,1)}, bf16[3,192,768]{2,1,0:T(8,128)(2,1)}, bf16[3,192,768]{2,1,0:T(8,128)(2,1)}), (bf16[3,192,768]{2,1,0:T(8,128)(2,1)}, bf16[3,192,768]{2,1,0:T(8,128)(2,1)}, ...) | async-done | bytes 2654224 | tf_op jit(solution)/shard_map/psum | solution.py:96
  547.5 3.9 fusion.13
  551.4 2.8 fusion.26
  555.9 3.7 all-to-all-start.2
  559.6 4.3 fusion.3
  564.0 2.9 convolution_bitcast_fusion.1
  566.9 4.3 fusion.27
  571.2 1.7 copy.109
  575.6 2.7 convolution_bitcast_fusion.2
  578.4 3.6 copy-done.5
  583.8 4.5 all-to-all-done.2
  588.3 3.5 all-to-all-start.6
  591.9 3.0 convolution_bitcast_fusion
  594.9 3.7 copy-done.2
  601.4 1.9 copy.123
  603.3 3.8 reshape.112
  607.1 12.8 %all-to-all-done.6 = bf16[8,3,24,1024]{3,0,1,2:T(8,128)(2,1)S(1)} async-done(((bf16[8,3,24,1024]{3,0,1,2:T(8,128)(2,1)}), bf16[8,3,24,1024]{3,0,1,2:T(8,128)(2,1)S(1)}, u32[]{:S(2)}, u32[]{:S(2)}) %all-to-all-start.6) | async-done | bytes 1179680 | tf_op jit(solution)/shard_map/all_to_all | solution.py:157
  619.9 4.5 all-to-all-start.3
  624.6 1.8 convert_element_type.141
  626.4 27.5 %collective-permute-done.3 = bf16[1024,768]{1,0:T(8,128)(2,1)} collective-permute-done((bf16[1024,768]{1,0:T(8,128)(2,1)}, bf16[1024,768]{1,0:T(8,128)(2,1)}, u32[]{:S(2)}, u32[]{:S(2)}) %collective-permute-start.3) | collective-permute-done | bytes 1572896 | tf_op jit(solution)/shard_map/ppermute | solution.py:9
  653.9 3.3 convert_element_type.138
  657.2 30.4 %collective-permute-done.5 = bf16[768,1024]{1,0:T(8,128)(2,1)} collective-permute-done((bf16[768,1024]{1,0:T(8,128)(2,1)}, bf16[768,1024]{1,0:T(8,128)(2,1)}, u32[]{:S(2)}, u32[]{:S(2)}) %collective-permute-start.5) | collective-permute-done | bytes 1572896 | tf_op jit(solution)/shard_map/ppermute | solution.py:9
  687.6 1.8 convert_element_type.144
  689.4 3.1 fusion
  692.5 1.9 copy.126
  694.5 3.9 reshape.114
  698.3 4.3 all-to-all-start.7
  702.6 9.1 %fusion.1 = (bf16[2,1024,768]{2,1,0:T(8,128)(2,1)}, bf16[2,1024,768]{2,1,0:T(8,128)(2,1)}) fusion(f32[3,1024,768]{2,1,0:T(8,128)} %copy-done.4, f32[1024,768]{1,0:T(8,128)S(1)} %convert_element_type.141, f32[2]{0:T(128)S(1)} %compare_convert_fusion, f32[1024,768]{1,0:T(8,128)} %convert_element_type.138, f32[3,1024,768]{2,1,0:T(8,128)} %copy-done.5), kind=kLoop, calls=%fused_computation.3 | loop fusion | flops 9437184 | bytes 25165832 | tf_op jit(solution)/shard_map/convert_element_type | solution.py:146
  713.3 1.7 multiply_reduce_fusion
  714.9 8.7 %all-to-all-done.7 = bf16[8,3,6,4096]{3,2,1,0:T(8,128)(2,1)} async-done(((bf16[8,3,6,4096]{3,2,1,0:T(8,128)(2,1)}), bf16[8,3,6,4096]{3,2,1,0:T(8,128)(2,1)}, u32[]{:S(2)}, u32[]{:S(2)}) %all-to-all-start.7) | async-done | bytes 1179680 | tf_op jit(solution)/shard_map/all_to_all | solution.py:156
  (80 shorter events, 30.2 us)
Async XLA Ops:
  7.2 1.4 copy-start
  100.2 6.5 copy-start.15
  100.2 6.5 copy-start.16
  100.2 100.9 %all-to-all-start = ((bf16[4,2,73728]{2,1,0:T(2,128)(2,1)}), bf16[4,2,73728]{2,1,0:T(2,128)(2,1)S(1)}, u32[]{:S(2)}, u32[]{:S(2)}) async-start(bf16[4,2,73728]{2,1,0:T(2,128)(2,1)} %reshape.116), calls=%async_computation | async-start | bytes 2359296 | tf_op jit(solution)/shard_map/all_to_all | solution.py:67
  201.1 5.1 copy-start.17
  201.1 107.7 %all-to-all-start.4 = ((bf16[4,2,73728]{2,1,0:T(2,128)(2,1)}), bf16[4,2,73728]{2,1,0:T(2,128)(2,1)S(1)}, u32[]{:S(2)}, u32[]{:S(2)}) async-start(bf16[4,2,73728]{2,1,0:T(2,128)(2,1)} %reshape.118), calls=%async_computation.4 | async-start | bytes 2359296 | tf_op jit(solution)/shard_map/all_to_all | solution.py:74
  210.1 210.0 %collective-permute-start.2 = (bf16[1024,768]{1,0:T(8,128)(2,1)}, bf16[1024,768]{1,0:T(8,128)(2,1)}, u32[]{:S(2)}, u32[]{:S(2)}) collective-permute-start(bf16[1024,768]{1,0:T(8,128)(2,1)} %dynamic-slice_bitcast_fusion), channel_id=1, source_target_pairs={{0,4},{1,5},{2,6},{3,7},{4,0},{5,1},{6,2},{7,3},{8,12},{9,13},{10,... | collective-permute-start | bytes 4718600 | tf_op jit(solution)/shard_map/ppermute | solution.py:9
  308.8 107.2 %all-to-all-start.1 = ((bf16[8,3,24,1024]{3,2,1,0:T(8,128)(2,1)}), bf16[8,3,24,1024]{3,2,1,0:T(8,128)(2,1)}, u32[]{:S(2)}, u32[]{:S(2)}) async-start(bf16[8,3,24,1024]{3,2,1,0:T(8,128)(2,1)} %copy.96), calls=%async_computation.1 | async-start | bytes 2359296 | tf_op jit(solution)/shard_map/all_to_all | solution.py:66
  313.3 3.7 copy-start.11
  314.9 110.1 %collective-permute-start.1 = (bf16[1024,768]{1,0:T(8,128)(2,1)S(1)}, bf16[1024,768]{1,0:T(8,128)(2,1)}, u32[]{:S(2)}, u32[]{:S(2)}) collective-permute-start(bf16[1024,768]{1,0:T(8,128)(2,1)S(1)} %dynamic-slice_bitcast_fusion.1), channel_id=1, source_target_pairs={{0,4},{1,5},{2,6},{3,7},{4,0},{5,1},{6,2},{7,3},{8,12},{9,13},{10,... | collective-permute-start | bytes 4718600 | tf_op jit(solution)/shard_map/ppermute | solution.py:9
  318.3 110.7 %collective-permute-start = (bf16[768,1024]{1,0:T(8,128)(2,1)}, bf16[768,1024]{1,0:T(8,128)(2,1)}, u32[]{:S(2)}, u32[]{:S(2)}) collective-permute-start(bf16[768,1024]{1,0:T(8,128)(2,1)} %dynamic-slice_bitcast_fusion.2), channel_id=1, source_target_pairs={{0,4},{1,5},{2,6},{3,7},{4,0},{5,1},{6,2},{7,3},{8,12},{9,13},{10,... | collective-permute-start | bytes 4718600 | tf_op jit(solution)/shard_map/ppermute | solution.py:9
  416.0 20.4 %all-to-all-start.5 = ((bf16[8,3,24,1024]{3,2,1,0:T(8,128)(2,1)}), bf16[8,3,24,1024]{3,2,1,0:T(8,128)(2,1)S(1)}, u32[]{:S(2)}, u32[]{:S(2)}) async-start(bf16[8,3,24,1024]{3,2,1,0:T(8,128)(2,1)} %copy.107), calls=%async_computation.5 | async-start | bytes 2359296 | tf_op jit(solution)/shard_map/all_to_all | solution.py:73
  419.6 127.9 %all-reduce.3.cloned.1.call-start = ((), (), s32[]{:S(2)}) async-start(), calls=%async_computation.8 | async-start | bytes 5308416 | tf_op jit(solution)/shard_map/psum | solution.py:96
  420.1 5.0 copy-start.13
  436.4 5.4 copy-start.8
  547.5 3.9 copy-start.12
  551.4 2.8 copy-start.9
  555.9 32.4 %all-to-all-start.2 = ((bf16[8,3,24,1024]{3,0,1,2:T(8,128)(2,1)}), bf16[8,3,24,1024]{3,0,1,2:T(8,128)(2,1)S(1)}, u32[]{:S(2)}, u32[]{:S(2)}) async-start(bf16[8,3,24,1024]{3,0,1,2:T(8,128)(2,1)} %copy.99), calls=%async_computation.2 | async-start | bytes 2359296 | tf_op jit(solution)/shard_map/all_to_all | solution.py:104
  559.6 4.4 copy-start.10
  564.0 2.9 copy-start.14
  566.9 6.0 copy-start.4
  574.2 50.4 %collective-permute-start.4 = (bf16[1024,768]{1,0:T(8,128)(2,1)}, bf16[1024,768]{1,0:T(8,128)(2,1)}, u32[]{:S(2)}, u32[]{:S(2)}) collective-permute-start(bf16[1024,768]{1,0:T(8,128)(2,1)} %fusion.20), channel_id=1, source_target_pairs={{0,4},{1,5},{2,6},{3,7},{4,0},{5,1},{6,2},{7,3},{8,12},{9,13},{10,... | collective-permute-start | bytes 4718600 | tf_op jit(solution)/shard_map/ppermute | solution.py:9
  578.4 3.6 copy-start.5
  583.3 70.6 %collective-permute-start.3 = (bf16[1024,768]{1,0:T(8,128)(2,1)}, bf16[1024,768]{1,0:T(8,128)(2,1)}, u32[]{:S(2)}, u32[]{:S(2)}) collective-permute-start(bf16[1024,768]{1,0:T(8,128)(2,1)} %fusion.19), channel_id=1, source_target_pairs={{0,4},{1,5},{2,6},{3,7},{4,0},{5,1},{6,2},{7,3},{8,12},{9,13},{10,... | collective-permute-start | bytes 4718600 | tf_op jit(solution)/shard_map/ppermute | solution.py:9
  588.3 31.6 %all-to-all-start.6 = ((bf16[8,3,24,1024]{3,0,1,2:T(8,128)(2,1)}), bf16[8,3,24,1024]{3,0,1,2:T(8,128)(2,1)S(1)}, u32[]{:S(2)}, u32[]{:S(2)}) async-start(bf16[8,3,24,1024]{3,0,1,2:T(8,128)(2,1)} %copy.109), calls=%async_computation.6 | async-start | bytes 2359296 | tf_op jit(solution)/shard_map/all_to_all | solution.py:157
  594.9 3.7 copy-start.2
  599.9 87.7 %collective-permute-start.5 = (bf16[768,1024]{1,0:T(8,128)(2,1)}, bf16[768,1024]{1,0:T(8,128)(2,1)}, u32[]{:S(2)}, u32[]{:S(2)}) collective-permute-start(bf16[768,1024]{1,0:T(8,128)(2,1)} %fusion.21), channel_id=1, source_target_pairs={{0,4},{1,5},{2,6},{3,7},{4,0},{5,1},{6,2},{7,3},{8,12},{9,13},{10,... | collective-permute-start | bytes 4718600 | tf_op jit(solution)/shard_map/ppermute | solution.py:9
  619.9 4.6 copy-start.6
  619.9 78.4 %all-to-all-start.3 = ((bf16[8,3,6,4096]{3,2,1,0:T(8,128)(2,1)}), bf16[8,3,6,4096]{3,2,1,0:T(8,128)(2,1)}, u32[]{:S(2)}, u32[]{:S(2)}) async-start(bf16[8,3,6,4096]{3,2,1,0:T(8,128)(2,1)} %reshape.112), calls=%async_computation.3 | async-start | bytes 3145728 | tf_op jit(solution)/shard_map/all_to_all | solution.py:103
  624.6 64.9 %copy-start.3 = (f32[3,768,1024]{2,1,0:T(8,128)S(1)}, f32[3,768,1024]{2,1,0:T(8,128)}, u32[]{:S(2)}) copy-start(f32[3,768,1024]{2,1,0:T(8,128)} %copy-done.2) | copy-start | bytes 28311556
  689.4 3.1 copy-start.7
  698.3 25.3 %all-to-all-start.7 = ((bf16[8,3,6,4096]{3,2,1,0:T(8,128)(2,1)}), bf16[8,3,6,4096]{3,2,1,0:T(8,128)(2,1)}, u32[]{:S(2)}, u32[]{:S(2)}) async-start(bf16[8,3,6,4096]{3,2,1,0:T(8,128)(2,1)} %reshape.114), calls=%async_computation.7 | async-start | bytes 3145728 | tf_op jit(solution)/shard_map/all_to_all | solution.py:156
  713.3 14.1 %copy-start.1 = (bf16[16,4096]{1,0:T(8,128)(2,1)S(1)}, bf16[16,4096]{1,0:T(8,128)(2,1)}, u32[]{:S(2)}) copy-start(bf16[16,4096]{1,0:T(8,128)(2,1)} %param.8) | copy-start | bytes 393220
Sparse Core Ops, SparseCore 0:
  442.0 105.4 all-reduce.2
where the time goes:
time: 748 us; the launch traced here: 734 us
  local copies, waits for them, and re-layouts  415 us (55%)
  waiting for transfers between devices  197 us (26%)
  starting transfers between devices  43.8 us (6%)
  matrix products  39.4 us (5%)
  other arithmetic  23.4 us (3%)
  between operations  15.3 us (2%)
    unnamed x43, local copies, waits for them, and re-layouts  287 us
    psum x1, waiting for transfers between devices, local(): lax.psum(partial_up.astype(jnp.bfloat16), 'dp').astype(jnp.float32)  106 us
    ppermute x6, waiting for transfers between devices, passed_along(): lax.ppermute(array, axis, [(i, (i + by) % length) for i in range(length)])  57.9 us
    all_to_all x3, local copies, waits for them, and re-layouts, local(): lax.all_to_all(send_scaled, 'dp', split_axis=3, concat_axis=2, tiled=True)  27.9 us
    all_to_all x3, local copies, waits for them, and re-layouts, local(): lax.all_to_all(send_rows, 'dp', split_axis=3, concat_axis=2, tiled=True)  27.9 us
    reshape x2, local copies, waits for them, and re-layouts, local(): send_scaled = send_scaled.reshape(owners, per_unit, capacity, model_width)  22.8 us
    reshape x2, local copies, waits for them, and re-layouts, local(): send_rows = send_rows.reshape(owners, per_unit, capacity, model_width)  21.8 us
  transfers between devices with their start and end apart: 15, of which 7 were waited for; matrix products, arithmetic and copies ran while one was open for 49% of the time, Pallas kernels for 0%

commit v1 on v0

v1 whole, which is shorter than its diff:
```python
import jax
import jax.numpy as jnp
from jax import lax
from jax.sharding import PartitionSpec as P

BF = jnp.bfloat16
F32 = jnp.float32


def dot(spec, a, b):
    return jnp.einsum(spec, a, b, preferred_element_type=F32)


def local(tokens, units, replicas, route_probs, cotangent, w_gate, w_up, w_down):
    groups = lax.axis_size("dp")
    owners = lax.axis_size("expert")
    per_owner = w_gate.shape[0]
    per_unit = per_owner + 1
    unit_total = per_unit * owners
    tok = units.shape[0]
    top = units.shape[1]
    blocks = groups * owners
    total = blocks * tok
    cap = (tok * top + unit_total - 1) // unit_total
    slots = blocks * cap
    width = w_gate.shape[1]
    half = owners // 2
    me = lax.axis_index("expert")
    my_group = lax.axis_index("dp")
    host = (me + half) % owners
    lent = replicas[host] - me * per_owner

    routing = jnp.concatenate([units.astype(F32), route_probs], axis=1)
    routing = lax.all_gather(routing, ("dp", "expert"), axis=0, tiled=True)
    routing = routing.reshape(groups, owners, tok, 2 * top).transpose(1, 0, 2, 3)
    routing = routing.reshape(total, 2 * top)
    all_units = routing[:, :top].astype(jnp.int32)
    all_probs = routing[:, top:]
    both = jnp.concatenate([tokens, cotangent], axis=0)
    both = lax.all_to_all(both, "dp", split_axis=1, concat_axis=0, tiled=True)
    both = lax.all_gather(both, "expert", axis=0, tiled=True)
    both = both.reshape(blocks, 2, tok, width)
    all_tokens = both[:, 0].reshape(total, width)
    all_cot = both[:, 1].reshape(total, width)

    mine = jnp.concatenate(
        [
            me * per_unit + jnp.arange(per_owner, dtype=jnp.int32),
            (host * per_unit + per_owner)[None].astype(jnp.int32),
        ]
    )
    match = all_units[None] == mine[:, None, None]
    named = jnp.any(match, axis=2)
    unit_probs = jnp.sum(jnp.where(match, all_probs[None], 0.0), axis=2)
    by_block = named.reshape(per_unit, blocks, tok).astype(jnp.int32)
    earlier = (
        jnp.arange(tok, dtype=jnp.int32)[:, None] < jnp.arange(tok, dtype=jnp.int32)[None, :]
    ).astype(jnp.int32)
    rank = jnp.sum(by_block[:, :, :, None] * earlier, axis=2)
    slot = (rank + jnp.arange(blocks, dtype=jnp.int32)[None, :, None] * cap).reshape(
        per_unit, total
    )
    slot = jnp.where(named, slot, -1)
    chosen = slot[:, None, :] == jnp.arange(slots, dtype=jnp.int32)[None, :, None]
    select = chosen.astype(BF)
    slot_probs = jnp.sum(jnp.where(chosen, unit_probs[:, None, :], 0.0), axis=2)

    flat_select = select.reshape(per_unit * slots, total)
    xs = dot("st,td->sd", flat_select, all_tokens).astype(BF).reshape(per_unit, slots, width)
    ds = (
        slot_probs.reshape(-1)[:, None] * dot("st,td->sd", flat_select, all_cot)
    ).astype(BF).reshape(per_unit, slots, width)

    def at(weights, u):
        if u < per_owner:
            return weights[u]
        return lax.dynamic_index_in_dim(weights, lent, 0, keepdims=False)

    def per(spec, rows, weights):
        return jnp.stack(
            [dot(spec, rows[u], at(weights, u)).astype(BF) for u in range(per_unit)]
        )

    gate, up, grad_hidden = lax.psum(
        (
            per("sd,df->sf", xs, w_gate),
            per("sd,df->sf", xs, w_up),
            per("sd,fd->sf", ds, w_down),
        ),
        "dp",
    )
    gate, up, grad_hidden = gate.astype(F32), up.astype(F32), grad_hidden.astype(F32)
    sig = jax.nn.sigmoid(gate)
    silu = gate * sig
    hidden = (silu * up).astype(BF)
    grad_gate = (grad_hidden * up * sig * (1.0 + gate * (1.0 - sig))).astype(BF)
    grad_up = (grad_hidden * silu).astype(BF)

    def send_back(rows):
        part = dot("st,sd->td", flat_select, rows.reshape(per_unit * slots, width)).astype(BF)
        part = lax.all_to_all(part, "expert", split_axis=0, concat_axis=0, tiled=True)
        part = part.reshape(owners, groups, tok, width)
        return jnp.sum(part.astype(F32), axis=0).astype(BF)

    expert_out = jnp.stack([dot("sf,fd->sd", hidden[u], at(w_down, u)) for u in range(per_unit)])
    out_part = send_back((slot_probs[:, :, None] * expert_out).astype(BF))
    expert_grad = jnp.stack(
        [
            (
                dot("sf,df->sd", grad_gate[u], at(w_gate, u))
                + dot("sf,df->sd", grad_up[u], at(w_up, u))
            ).astype(BF)
            for u in range(per_unit)
        ]
    )
    grad_part = send_back(expert_grad)
    last = jnp.concatenate([out_part, grad_part], axis=1).reshape(groups * 2 * tok, width)
    last = lax.all_to_all(last, "dp", split_axis=0, concat_axis=1, tiled=True)
    layer_out = last[:tok]
    d_tokens = last[tok:]

    filled = slot_probs > 0.0
    dots = jnp.sum(hidden.astype(F32) * grad_hidden, axis=2) / jnp.where(filled, slot_probs, 1.0)
    per_token = jnp.sum(jnp.where(chosen, dots[:, :, None], 0.0), axis=1)
    spread = jnp.sum(jnp.where(match, per_token[:, :, None], 0.0), axis=0)
    spread = lax.dynamic_index_in_dim(
        spread.reshape(owners, groups, tok, top), my_group, 1, keepdims=False
    )
    spread = lax.all_to_all(spread, "expert", split_axis=0, concat_axis=0, tiled=True)
    d_probs = jnp.sum(spread, axis=0)

    def weight_grads(left, right):
        grads = []
        for e in range(per_owner):
            marked = jnp.where(lent == e, 1.0, 0.0).astype(BF)
            a = jnp.concatenate([left[e], left[per_owner]], axis=0)
            b = jnp.concatenate([right[e], right[per_owner] * marked], axis=0)
            grads.append(dot("sa,sb->ab", a, b).astype(BF))
        return jnp.stack(grads)

    d_gate_w = weight_grads(xs, grad_gate)
    d_up_w = weight_grads(xs, grad_up)
    d_down_w = weight_grads(hidden, ds)
    return (layer_out, d_tokens, d_probs, d_gate_w, d_up_w, d_down_w)


def solution(mesh):
    rows = P(("dp", "expert"), None)
    weights = P("expert", "dp", None)
    down = P("expert", None, "dp")
    return jax.shard_map(
        local,
        mesh=mesh,
        in_specs=(rows, rows, P(), rows, rows, weights, weights, down),
        out_specs=(rows, rows, rows, weights, weights, down),
        check_vma=False,
    )
```

time: 748 us -> 268 us (0.36); the launches traced: 734 us -> 268 us
  local copies, waits for them, and re-layouts: 415 us -> 15 us
  waiting for transfers between devices: 197 us -> 110 us
  blocking collectives: 0 us -> 55.5 us
  starting transfers between devices: 43.8 us -> 15.3 us
    unnamed x43 -> x77, local copies, waits for them, and re-layouts: 287 us -> 4.75 us
    all_to_all x10 -> x2, local copies, waits for them, and re-layouts: 67.3 us -> 0.53 us  [the longest x1 0.51 us: local(): lax.all_to_all(spread, 'expert', split_axis=0, concat_axis=0, tiled=True)]
    ppermute x6 -> x0, waiting for transfers between devices: 57.9 us -> none  [passed_along(): lax.ppermute(array, axis, [(i, (i + by) % length) for i in range(length)])]
    reshape x7 -> x3, local copies, waits for them, and re-layouts: 47.9 us -> 0.67 us  [the longest x1 0.29 us: local(): routing.reshape(groups, owners, tok, 2 * top).transpose(1, 0, 2, 3)]
    all_gather x0 -> x1, blocking collectives: none -> 40.4 us  [local(): routing = lax.all_gather(routing, ('dp', 'expert'), axis=0, tiled=True)]
    convert_element_type x9 -> x3, other arithmetic: 23.1 us -> 0.02 us  [the longest x1 0.01 us: local(): by_block = named.reshape(per_unit, blocks, tok).astype(jnp.int32)]
    all_to_all x8 -> x4, waiting for transfers between devices: 33.5 us -> 10.6 us  [the longest x2 3.84 us: send_back(): lax.all_to_all(part, 'expert', split_axis=0, concat_axis=0, tiled=True)]
    all_to_all x8 -> x4, starting transfers between devices: 35.7 us -> 15.2 us  [the longest x2 8.46 us: send_back(): lax.all_to_all(part, 'expert', split_axis=0, concat_axis=0, tiled=True)]
  transfers between devices with their start and end apart: 15 -> 6, of which waited for: 7 -> 4; matrix products, arithmetic and copies ran while one was open for 49% -> 16% of each run, Pallas kernels for 0% -> 0%
where the time goes in v1:
time: 268 us
  waiting for transfers between devices  110 us (41%)
  blocking collectives  55.5 us (21%)
  matrix products  35 us (13%)
  other arithmetic  21.8 us (8%)
  between operations  15.4 us (6%)
  starting transfers between devices  15.3 us (6%)
  local copies, waits for them, and re-layouts  15 us (6%)
    psum x1, waiting for transfers between devices, local(): lax.psum((per('sd,df->sf', xs, w_gate), per('sd,df->sf', xs, w_up), per('...  98.9 us
    all_gather x1, blocking collectives, local(): routing = lax.all_gather(routing, ('dp', 'expert'), axis=0, tiled=True)  40.4 us
    dot_general x28, matrix products, dot(): return jnp.einsum(spec, a, b, preferred_element_type=F32)  35 us
    all_to_all x1, blocking collectives, local(): both = lax.all_to_all(both, 'dp', split_axis=1, concat_axis=0, tiled=True)  15.1 us
    all_to_all x2, starting transfers between devices, send_back(): lax.all_to_all(part, 'expert', split_axis=0, concat_axis=0, tiled=True)  8.46 us
    another operation x3, other arithmetic, weight_grads(): return jnp.stack(grads)  7.31 us
  transfers between devices with their start and end apart: 6, of which 4 were waited for; matrix products, arithmetic and copies ran while one was open for 16% of the time, Pallas kernels for 0%

profile of v1, /device:TPU:0, one launch (start us, length us, event | category | flops | bytes accessed | tf_op | source)
XLA Modules:
  0.0 267.6 jit_solution(3367294730793408145)
XLA Ops:
  7.2 1.0 pad_maximum_fusion.13
  8.3 15.1 %all_to_all.55 = bf16[32,4,1024]{2,0,1:T(8,128)(2,1)} all-to-all(bf16[32,4,1024]{2,0,1:T(8,128)(2,1)S(1)} %bitcast.234), channel_id=1, replica_groups=mesh['dp'=4,'expert'=8] {'dp'}, dimensions={1} | all-to-all | bytes 524288 | tf_op jit(solution)/shard_map/all_to_all | solution.py:40
  25.0 40.4 %all_gather.6 = f32[512,16]{1,0:T(8,128)S(1)} all-gather(f32[16,16]{1,0:T(8,128)S(1)} %copy.57), channel_id=1, replica_groups=mesh['dp'=4,'expert'=8] {'dp','expert'}, dimensions={0}, use_global_device_ids=true | all-gather | bytes 33792 | tf_op jit(solution)/shard_map/all_gather | solution.py:34
  67.3 1.7 fusion.224
  69.0 0.8 convolution_convert_fusion.6
  69.8 1.1 copy-done.6
  72.4 0.9 copy-done
  74.8 0.8 multiply_convert_fusion
  75.6 1.1 copy-done.4
  77.3 0.7 fusion.141
  78.7 1.0 pad_maximum_fusion.5
  79.7 1.4 pad_maximum_fusion.3
  81.2 2.1 fusion.226
  83.3 1.1 fusion.225
  84.4 98.9 %all-reduce.3.cloned.1.call-done = (bf16[3,192,768]{2,1,0:T(8,128)(2,1)}, bf16[3,192,768]{2,1,0:T(8,128)(2,1)}, bf16[3,192,768]{2,1,0:T(8,128)(2,1)}) async-done(((bf16[3,192,768]{2,1,0:T(8,128)(2,1)}, bf16[3,192,768]{2,1,0:T(8,128)(2,1)}, bf16[3,192,768]{2,1,0:T(8,128)(2,1)}), (bf16[3,192,768]{2,1,0:T(8,128)(2,1)}, bf16[3,192,768]{2,1,0:T(8,128)(2,1)}, ...) | async-done | bytes 2654224 | tf_op jit(solution)/shard_map/psum | solution.py:84
  183.3 3.0 %fusion.10 = (f32[3,192]{1,0:T(4,128)S(1)}, bf16[3,192,768]{2,1,0:T(8,128)(2,1)S(1)}, bf16[3,192,768]{2,1,0:T(8,128)(2,1)S(1)}, bf16[3,192,768]{2,1,0:T(8,128)(2,1)S(1)}) fusion(bf16[3,192,768]{2,1,0:T(8,128)(2,1)} %get-tuple-element.6, bf16[3,192,768]{2,1,0:T(8,128)(2,1)} %get-tuple-element.8, bf16[3,192,768]{2,1,0:T(8,128)(2,1)} %get-tuple-element.7), kind=kLoop, calls=%fused_computation.24 | loop fusion | flops 9289152 | bytes 5310720 | tf_op jit(solution)/shard_map/reduce_sum | solution.py:123
  186.3 0.9 fusion.196
  187.3 0.8 slice_bitcast_fusion.5
  189.6 1.0 slice_bitcast_fusion.8
  190.6 0.7 copy-done.7
  191.3 1.5 fusion.31
  192.9 1.6 fusion.23
  195.4 2.1 bitcast_convert_fusion.1
  197.4 4.4 %all-to-all-start.1 = ((bf16[8,64,1024]{2,1,0:T(8,128)(2,1)}), bf16[8,64,1024]{2,1,0:T(8,128)(2,1)}, u32[]{:S(2)}, u32[]{:S(2)}) async-start(bf16[8,64,1024]{2,1,0:T(8,128)(2,1)} %bitcast.231), calls=%async_computation.1 | async-start | bytes 2097152 | tf_op jit(solution)/shard_map/all_to_all | solution.py:101
  201.9 2.7 %fusion.125 = bf16[1,192,1024]{2,1,0:T(8,128)(2,1)} fusion(f32[192,1024]{1,0:T(8,128)} %fusion.31, bf16[2,1024,768]{2,1,0:T(8,128)(2,1)S(1)} %copy-done, bf16[3,192,768]{2,1,0:T(8,128)(2,1)} %copy-done.1), kind=kOutput, calls=%fused_computation.110 | convolution fusion | flops 302383104 | bytes 3047424 | tf_op jit(solution)/shard_map/sf,df->sd/dot_general | solution.py:11
  204.6 2.5 fusion.131
  207.1 1.0 fusion.51
  208.2 1.0 fusion.52
  209.3 1.9 pad_maximum_fusion.2
  211.2 2.2 fusion.48
  213.6 2.2 fusion.27
  215.8 1.7 fusion.128
  217.5 2.0 bitcast_convert_fusion
  219.5 4.0 %all-to-all-start.2 = ((bf16[8,64,1024]{2,1,0:T(8,128)(2,1)}), bf16[8,64,1024]{2,1,0:T(8,128)(2,1)S(1)}, u32[]{:S(2)}, u32[]{:S(2)}) async-start(bf16[8,64,1024]{2,1,0:T(8,128)(2,1)} %bitcast.47), calls=%async_computation.2 | async-start | bytes 2097152 | tf_op jit(solution)/shard_map/all_to_all | solution.py:101
  223.6 3.5 %fusion.47 = bf16[1,1024,768]{2,1,0:T(8,128)(2,1)} fusion(bf16[192,768]{1,0:T(8,128)(2,1)} %get-tuple-element.30, bf16[192,768]{1,0:T(8,128)(2,1)} %get-tuple-element.28, bf16[192,1024]{1,0:T(8,128)(2,1)} %get-tuple-element.20, bf16[192,1024]{1,0:T(8,128)(2,1)S(1)} %copy-done.20), kind=kOutput, calls=%fused_computation.68 | convolution fusion | flops 607518720 | bytes 2949120 | tf_op jit(solution)/shard_map/sa,sb->ab/dot_general | solution.py:11
  227.8 3.4 %pad_maximum_fusion = bf16[2,1024,768]{2,1,0:T(8,128)(2,1)} fusion(bf16[1,1024,768]{2,1,0:T(8,128)(2,1)S(1)} %copy-done.14, bf16[1,1024,768]{2,1,0:T(8,128)(2,1)} %fusion.47), kind=kLoop, calls=%fused_computation | loop fusion | flops 1572864 | bytes 6291456 | tf_op jit(solution)/shard_map/stack | solution.py:139
  231.2 0.8 fusion.198
  232.0 0.7 slice_bitcast_fusion.4
  232.7 1.0 fusion.50
  233.7 1.4 reduce_sum.97
  235.1 3.8 %all-to-all-done.2 = bf16[8,64,1024]{2,1,0:T(8,128)(2,1)S(1)} async-done(((bf16[8,64,1024]{2,1,0:T(8,128)(2,1)}), bf16[8,64,1024]{2,1,0:T(8,128)(2,1)S(1)}, u32[]{:S(2)}, u32[]{:S(2)}) %all-to-all-start.2) | async-done | bytes 1048608 | tf_op jit(solution)/shard_map/all_to_all | solution.py:101
  239.0 3.3 %all-to-all-start.4 = ((f32[8,1,128]{2,1,0:T(1,128)}), f32[8,1,128]{2,1,0:T(1,128)S(1)}, u32[]{:S(2)}, u32[]{:S(2)}) async-start(f32[8,1,128]{2,1,0:T(1,128)} %reshape.188), calls=%async_computation.4 | async-start | bytes 8192 | tf_op jit(solution)/shard_map/all_to_all | solution.py:129
  242.5 0.7 pad_maximum_fusion.14
  243.2 3.6 %all-to-all-done.4 = f32[8,1,128]{2,1,0:T(1,128)S(1)} async-done(((f32[8,1,128]{2,1,0:T(1,128)}), f32[8,1,128]{2,1,0:T(1,128)S(1)}, u32[]{:S(2)}, u32[]{:S(2)}) %all-to-all-start.4) | async-done | bytes 4128 | tf_op jit(solution)/shard_map/all_to_all | solution.py:129
  246.8 3.4 %all-to-all-start.3 = ((bf16[4,32,1024]{2,1,0:T(8,128)(2,1)}), bf16[4,32,1024]{2,1,0:T(8,128)(2,1)S(1)}, u32[]{:S(2)}, u32[]{:S(2)}) async-start(bf16[4,32,1024]{2,1,0:T(8,128)(2,1)} %pad_maximum_fusion.14), calls=%async_computation.3 | async-start | bytes 524288 | tf_op jit(solution)/shard_map/all_to_all | solution.py:118
  250.2 2.2 fusion.49
  252.4 1.9 pad_maximum_fusion.1
  256.2 3.1 %all-to-all-done.3 = bf16[4,32,1024]{2,1,0:T(8,128)(2,1)S(1)} async-done(((bf16[4,32,1024]{2,1,0:T(8,128)(2,1)}), bf16[4,32,1024]{2,1,0:T(8,128)(2,1)S(1)}, u32[]{:S(2)}, u32[]{:S(2)}) %all-to-all-start.3) | async-done | bytes 262176 | tf_op jit(solution)/shard_map/all_to_all | solution.py:118
  (128 shorter events, 13.7 us)
Async XLA Ops:
  7.2 16.3 %copy-start.36 = (s32[8]{0:T(128)S(1)}, s32[8]{0:T(128)}, u32[]{:S(2)}) copy-start(s32[8]{0:T(128)} %param.10) | copy-start | bytes 100
  7.2 17.5 %copy-start.34 = (s32[16,8]{0,1:T(8,128)S(1)}, s32[16,8]{0,1:T(8,128)}, u32[]{:S(2)}) copy-start(s32[16,8]{0,1:T(8,128)} %param.9) | copy-start | bytes 1540
  7.2 17.5 %copy-start.35 = (f32[16,8]{0,1:T(8,128)S(1)}, f32[16,8]{0,1:T(8,128)}, u32[]{:S(2)}) copy-start(f32[16,8]{0,1:T(8,128)} %param.11) | copy-start | bytes 1540
  7.2 60.0 %all-gather.2.cloned.1.call-start = ((), (), s32[]{:S(2)}) async-start(), calls=%async_computation.5 | async-start | bytes 2359296 | tf_op jit(solution)/shard_map/all_gather | solution.py:41
  23.4 159.9 %all-reduce.3.cloned.1.call-start = ((), (), s32[]{:S(2)}) async-start(), calls=%async_computation.6 | async-start | bytes 5308416 | tf_op jit(solution)/shard_map/psum | solution.py:84
  66.0 2.9 %copy-start.32 = (s32[3]{0:T(128)}, s32[3]{0:T(128)S(1)}, u32[]{:S(2)}) copy-start(s32[3]{0:T(128)S(1)} %pad_add_fusion) | copy-start | bytes 40
  66.8 2.2 copy-start.26
  67.0 2.0 copy-start.30
  69.0 1.9 copy-start.6
  70.9 3.4 %copy-start.11 = (bf16[576,1024]{1,0:T(8,128)(2,1)}, bf16[576,1024]{1,0:T(8,128)(2,1)S(1)}, u32[]{:S(2)}) copy-start(bf16[576,1024]{1,0:T(8,128)(2,1)S(1)} %convolution_convert_fusion.6) | copy-start | bytes 3538948
  71.4 1.9 copy-start
  74.8 1.9 copy-start.4
  76.6 1.4 copy-start.9
  81.2 2.2 copy-start.10
  183.3 4.8 %copy-start.5 = (bf16[2,768,1024]{2,1,0:T(8,128)(2,1)S(1)}, bf16[2,768,1024]{2,1,0:T(8,128)(2,1)}, u32[]{:S(2)}) copy-start(bf16[2,768,1024]{2,1,0:T(8,128)(2,1)} %param.15) | copy-start | bytes 9437188
  186.3 2.3 copy-start.1
  186.3 6.5 %copy-start.2 = (bf16[3,192,768]{2,1,0:T(8,128)(2,1)}, bf16[3,192,768]{2,1,0:T(8,128)(2,1)S(1)}, u32[]{:S(2)}) copy-start(bf16[3,192,768]{2,1,0:T(8,128)(2,1)S(1)} %get-tuple-element.14) | copy-start | bytes 2654212
  189.1 2.2 copy-start.7
  192.8 1.6 copy-start.31
  192.8 1.6 copy-start.27
  192.8 1.8 copy-start.33
  197.4 22.1 %all-to-all-start.1 = ((bf16[8,64,1024]{2,1,0:T(8,128)(2,1)}), bf16[8,64,1024]{2,1,0:T(8,128)(2,1)}, u32[]{:S(2)}, u32[]{:S(2)}) async-start(bf16[8,64,1024]{2,1,0:T(8,128)(2,1)} %bitcast.231), calls=%async_computation.1 | async-start | bytes 2097152 | tf_op jit(solution)/shard_map/all_to_all | solution.py:101
  201.9 2.7 %copy-start.8 = (f32[192,1024]{1,0:T(8,128)S(1)}, f32[192,1024]{1,0:T(8,128)}, u32[]{:S(2)}) copy-start(f32[192,1024]{1,0:T(8,128)} %fusion.23) | copy-start | bytes 2359300
  204.6 2.5 copy-start.16
  204.6 2.5 copy-start.17
  204.6 2.5 copy-start.21
  204.6 2.5 copy-start.23
  207.1 1.0 copy-start.15
  207.1 1.1 copy-start.22
  209.2 2.0 copy-start.12
  209.2 2.0 copy-start.24
  209.2 2.0 copy-start.25
  211.2 2.2 copy-start.29
  215.7 1.7 copy-start.18
  215.7 1.7 copy-start.19
  215.8 1.7 copy-start.28
  219.5 4.1 %copy-start.20 = (bf16[192,1024]{1,0:T(8,128)(2,1)S(1)}, bf16[192,1024]{1,0:T(8,128)(2,1)}, u32[]{:S(2)}) copy-start(bf16[192,1024]{1,0:T(8,128)(2,1)} %get-tuple-element.19) | copy-start | bytes 1179652
  219.5 19.5 %all-to-all-start.2 = ((bf16[8,64,1024]{2,1,0:T(8,128)(2,1)}), bf16[8,64,1024]{2,1,0:T(8,128)(2,1)S(1)}, u32[]{:S(2)}, u32[]{:S(2)}) async-start(bf16[8,64,1024]{2,1,0:T(8,128)(2,1)} %bitcast.47), calls=%async_computation.2 | async-start | bytes 2097152 | tf_op jit(solution)/shard_map/all_to_all | solution.py:101
  223.6 4.2 %copy-start.14 = (bf16[1,1024,768]{2,1,0:T(8,128)(2,1)S(1)}, bf16[1,1024,768]{2,1,0:T(8,128)(2,1)}, u32[]{:S(2)}) copy-start(bf16[1,1024,768]{2,1,0:T(8,128)(2,1)} %fusion.48) | copy-start | bytes 4718596
  227.8 3.4 %copy-start.3 = (bf16[3,192,768]{2,1,0:T(8,128)(2,1)S(1)}, bf16[3,192,768]{2,1,0:T(8,128)(2,1)}, u32[]{:S(2)}) copy-start(bf16[3,192,768]{2,1,0:T(8,128)(2,1)} %copy-done.2) | copy-start | bytes 2654212
  231.2 1.5 copy-start.13
  239.0 7.8 %all-to-all-start.4 = ((f32[8,1,128]{2,1,0:T(1,128)}), f32[8,1,128]{2,1,0:T(1,128)S(1)}, u32[]{:S(2)}, u32[]{:S(2)}) async-start(f32[8,1,128]{2,1,0:T(1,128)} %reshape.188), calls=%async_computation.4 | async-start | bytes 8192 | tf_op jit(solution)/shard_map/all_to_all | solution.py:129
  246.8 12.5 %all-to-all-start.3 = ((bf16[4,32,1024]{2,1,0:T(8,128)(2,1)}), bf16[4,32,1024]{2,1,0:T(8,128)(2,1)S(1)}, u32[]{:S(2)}, u32[]{:S(2)}) async-start(bf16[4,32,1024]{2,1,0:T(8,128)(2,1)} %pad_maximum_fusion.14), calls=%async_computation.3 | async-start | bytes 524288 | tf_op jit(solution)/shard_map/all_to_all | solution.py:118
Sparse Core Ops, SparseCore 0:
  23.5 27.6 all-gather.1
  81.3 101.9 all-reduce.2

commit v2 on v1

--- a/solution.py
+++ b/solution.py
@@ -38,10 +38,14 @@
     all_probs = routing[:, top:]
     both = jnp.concatenate([tokens, cotangent], axis=0)
     both = lax.all_to_all(both, "dp", split_axis=1, concat_axis=0, tiled=True)
-    both = lax.all_gather(both, "expert", axis=0, tiled=True)
-    both = both.reshape(blocks, 2, tok, width)
-    all_tokens = both[:, 0].reshape(total, width)
-    all_cot = both[:, 1].reshape(total, width)
+    both = both.reshape(groups, 2, tok, width)
+
+    def gathered(rows):
+        return lax.all_gather(rows.reshape(groups * tok, width), "expert", axis=0, tiled=True)
+
+    all_tokens = gathered(both[:, 0])
+    cot_rows, all_tokens = lax.optimization_barrier((both[:, 1], all_tokens))
+    all_cot = gathered(cot_rows)
 
     mine = jnp.concatenate(
         [
@@ -81,14 +85,9 @@
             [dot(spec, rows[u], at(weights, u)).astype(BF) for u in range(per_unit)]
         )
 
-    gate, up, grad_hidden = lax.psum(
-        (
-            per("sd,df->sf", xs, w_gate),
-            per("sd,df->sf", xs, w_up),
-            per("sd,fd->sf", ds, w_down),
-        ),
-        "dp",
-    )
+    gate, up = lax.psum((per("sd,df->sf", xs, w_gate), per("sd,df->sf", xs, w_up)), "dp")
+    partial_grad, gate, up = lax.optimization_barrier((per("sd,fd->sf", ds, w_down), gate, up))
+    grad_hidden = lax.psum(partial_grad, "dp")
     gate, up, grad_hidden = gate.astype(F32), up.astype(F32), grad_hidden.astype(F32)
     sig = jax.nn.sigmoid(gate)
     silu = gate * sig

time: 268 us -> 298 us (1.11)
  waiting for transfers between devices: 110 us -> 138 us
  matrix products: 35 us -> 39.9 us
  local copies, waits for them, and re-layouts: 15 us -> 11.2 us
    psum x1 -> x2, waiting for transfers between devices: 98.9 us -> 119 us  [the longest x1 73.7 us: local(): lax.psum((per('sd,df->sf', xs, w_gate), per('sd,df->sf', xs, w_up)), 'dp')]
    all_gather x1 -> x2, waiting for transfers between devices: 0.02 us -> 8.74 us  [gathered(): lax.all_gather(rows.reshape(groups * tok, width), 'expert', axis=0, tiled...]
    dot_general x28, matrix products: 35 us -> 39.9 us  [dot(): return jnp.einsum(spec, a, b, preferred_element_type=F32)]
  transfers between devices with their start and end apart: 6 -> 8, of which waited for: 4 -> 6; matrix products, arithmetic and copies ran while one was open for 16% -> 19% of each run, Pallas kernels for 0% -> 0%
where the time goes in v2:
time: 298 us
  waiting for transfers between devices  138 us (46%)
  blocking collectives  55.4 us (19%)
  matrix products  39.9 us (13%)
  other arithmetic  21.9 us (7%)
  starting transfers between devices  15.5 us (5%)
  between operations  15.1 us (5%)
  local copies, waits for them, and re-layouts  11.2 us (4%)
    psum x1, waiting for transfers between devices, local(): lax.psum((per('sd,df->sf', xs, w_gate), per('sd,df->sf', xs, w_up)), 'dp')  73.7 us
    psum x1, waiting for transfers between devices, local(): grad_hidden = lax.psum(partial_grad, 'dp')  45.5 us
    all_gather x1, blocking collectives, local(): routing = lax.all_gather(routing, ('dp', 'expert'), axis=0, tiled=True)  40.4 us
    dot_general x28, matrix products, dot(): return jnp.einsum(spec, a, b, preferred_element_type=F32)  39.9 us
    all_to_all x1, blocking collectives, local(): both = lax.all_to_all(both, 'dp', split_axis=1, concat_axis=0, tiled=True)  15 us
    all_gather x2, waiting for transfers between devices, gathered(): lax.all_gather(rows.reshape(groups * tok, width), 'expert', axis=0, tiled...  8.74 us
    all_to_all x2, starting transfers between devices, send_back(): lax.all_to_all(part, 'expert', split_axis=0, concat_axis=0, tiled=True)  8.48 us
    another operation x3, other arithmetic, weight_grads(): return jnp.stack(grads)  7.31 us
  transfers between devices with their start and end apart: 8, of which 6 were waited for; matrix products, arithmetic and copies ran while one was open for 19% of the time, Pallas kernels for 0%

profile of v2, /device:TPU:0, one launch (start us, length us, event | category | flops | bytes accessed | tf_op | source)
XLA Modules:
  0.0 297.6 jit_solution(11524022551701297620)
XLA Ops:
  7.2 1.0 pad_maximum_fusion.13
  8.3 15.0 %all_to_all.52 = bf16[32,4,1024]{2,0,1:T(8,128)(2,1)S(1)} all-to-all(bf16[32,4,1024]{2,0,1:T(8,128)(2,1)S(1)} %bitcast.235), channel_id=1, replica_groups=mesh['dp'=4,'expert'=8] {'dp'}, dimensions={1} | all-to-all | bytes 524288 | tf_op jit(solution)/shard_map/all_to_all | solution.py:40
  23.3 0.7 fusion.226
  24.3 40.4 %all_gather.9 = f32[512,16]{1,0:T(8,128)S(1)} all-gather(f32[16,16]{1,0:T(8,128)S(1)} %copy.62), channel_id=1, replica_groups=mesh['dp'=4,'expert'=8] {'dp','expert'}, dimensions={0}, use_global_device_ids=true | all-gather | bytes 33792 | tf_op jit(solution)/shard_map/all_gather | solution.py:34
  67.7 2.2 convolution_convert_fusion.6
  70.5 2.6 fusion.141
  75.0 1.4 pad_maximum_fusion.4
  77.2 8.7 %all-gather.5.cloned.1.call-done = bf16[512,1024]{1,0:T(8,128)(2,1)} async-done(((bf16[64,1024]{1,0:T(8,128)(2,1)}), bf16[512,1024]{1,0:T(8,128)(2,1)}) %all-gather.5.cloned.1.call-update) | async-done | bytes 1048592 | tf_op jit(solution)/shard_map/all_gather | solution.py:44
  85.9 2.2 multiply_convert_fusion
  90.1 1.0 pad_maximum_fusion.3
  91.1 73.7 %all-reduce.6.cloned.1.call-done = (bf16[3,192,768]{2,1,0:T(8,128)(2,1)}, bf16[3,192,768]{2,1,0:T(8,128)(2,1)}) async-done(((bf16[3,192,768]{2,1,0:T(8,128)(2,1)}, bf16[3,192,768]{2,1,0:T(8,128)(2,1)}), (bf16[3,192,768]{2,1,0:T(8,128)(2,1)}, bf16[3,192,768]{2,1,0:T(8,128)(2,1)})) %all-reduce.6.cloned.1.call-update) | async-done | bytes 1769488 | tf_op jit(solution)/shard_map/psum | solution.py:88
  164.9 2.2 fusion.225
  167.0 1.1 fusion.224
  168.1 45.5 %all-reduce.4.cloned.1.call-done = bf16[3,192,768]{2,1,0:T(8,128)(2,1)} async-done(((bf16[3,192,768]{2,1,0:T(8,128)(2,1)}), bf16[3,192,768]{2,1,0:T(8,128)(2,1)}) %all-reduce.4.cloned.1.call-update) | async-done | bytes 884752 | tf_op jit(solution)/shard_map/psum | solution.py:90
  213.6 3.0 %fusion.10 = (f32[3,192]{1,0:T(4,128)S(1)}, bf16[3,192,768]{2,1,0:T(8,128)(2,1)S(1)}, bf16[3,192,768]{2,1,0:T(8,128)(2,1)S(1)}, bf16[3,192,768]{2,1,0:T(8,128)(2,1)S(1)}) fusion(bf16[3,192,768]{2,1,0:T(8,128)(2,1)} %all-reduce.4.cloned.1.call-done, bf16[3,192,768]{2,1,0:T(8,128)(2,1)} %get-tuple-element.14, bf16[3,192,768]{2,1,0:T(8,128)(2,1)} %get-tuple-element.13), kind=kLoop, calls=%fused_computation.24 | loop fusion | flops 9289152 | bytes 5310720 | tf_op jit(solution)/shard_map/reduce_sum | solution.py:122
  216.6 0.9 fusion.196
  217.6 0.9 slice_bitcast_fusion.5
  219.9 1.0 slice_bitcast_fusion.8
  220.9 0.7 copy-done.7
  221.6 1.5 fusion.19
  223.2 1.6 fusion.11
  225.0 0.7 fusion.200
  225.7 2.1 bitcast_convert_fusion.1
  227.8 4.5 %all-to-all-start.1 = ((bf16[8,64,1024]{2,1,0:T(8,128)(2,1)}), bf16[8,64,1024]{2,1,0:T(8,128)(2,1)}, u32[]{:S(2)}, u32[]{:S(2)}) async-start(bf16[8,64,1024]{2,1,0:T(8,128)(2,1)} %bitcast.232), calls=%async_computation.1 | async-start | bytes 2097152 | tf_op jit(solution)/shard_map/all_to_all | solution.py:100
  232.2 2.7 fusion.125
  235.0 2.5 fusion.131
  237.5 1.0 fusion.51
  238.6 1.0 fusion.52
  239.6 1.9 pad_maximum_fusion.2
  241.6 2.2 fusion.48
  244.0 2.2 fusion.15
  246.2 1.7 fusion.128
  247.9 2.0 bitcast_convert_fusion
  249.9 4.0 %all-to-all-start.2 = ((bf16[8,64,1024]{2,1,0:T(8,128)(2,1)}), bf16[8,64,1024]{2,1,0:T(8,128)(2,1)S(1)}, u32[]{:S(2)}, u32[]{:S(2)}) async-start(bf16[8,64,1024]{2,1,0:T(8,128)(2,1)} %bitcast.48), calls=%async_computation.2 | async-start | bytes 2097152 | tf_op jit(solution)/shard_map/all_to_all | solution.py:100
  254.0 3.5 %fusion.47 = bf16[1,1024,768]{2,1,0:T(8,128)(2,1)} fusion(bf16[192,768]{1,0:T(8,128)(2,1)} %get-tuple-element.37, bf16[192,768]{1,0:T(8,128)(2,1)} %get-tuple-element.35, bf16[192,1024]{1,0:T(8,128)(2,1)} %get-tuple-element.27, bf16[192,1024]{1,0:T(8,128)(2,1)S(1)} %copy-done.20), kind=kOutput, calls=%fused_computation.68 | convolution fusion | flops 607518720 | bytes 2949120 | tf_op jit(solution)/shard_map/sa,sb->ab/dot_general | solution.py:11
  258.2 3.4 %pad_maximum_fusion = bf16[2,1024,768]{2,1,0:T(8,128)(2,1)} fusion(bf16[1,1024,768]{2,1,0:T(8,128)(2,1)S(1)} %copy-done.14, bf16[1,1024,768]{2,1,0:T(8,128)(2,1)} %fusion.47), kind=kLoop, calls=%fused_computation | loop fusion | flops 1572864 | bytes 6291456 | tf_op jit(solution)/shard_map/stack | solution.py:138
  261.6 0.8 fusion.198
  262.3 0.8 slice_bitcast_fusion.4
  263.1 1.0 fusion.50
  264.1 1.4 reduce_sum.97
  265.6 3.8 %all-to-all-done.2 = bf16[8,64,1024]{2,1,0:T(8,128)(2,1)S(1)} async-done(((bf16[8,64,1024]{2,1,0:T(8,128)(2,1)}), bf16[8,64,1024]{2,1,0:T(8,128)(2,1)S(1)}, u32[]{:S(2)}, u32[]{:S(2)}) %all-to-all-start.2) | async-done | bytes 1048608 | tf_op jit(solution)/shard_map/all_to_all | solution.py:100
  269.4 3.3 %all-to-all-start.4 = ((f32[8,1,128]{2,1,0:T(1,128)}), f32[8,1,128]{2,1,0:T(1,128)S(1)}, u32[]{:S(2)}, u32[]{:S(2)}) async-start(f32[8,1,128]{2,1,0:T(1,128)} %reshape.139), calls=%async_computation.4 | async-start | bytes 8192 | tf_op jit(solution)/shard_map/all_to_all | solution.py:128
  272.9 0.7 pad_maximum_fusion.14
  273.6 3.6 %all-to-all-done.4 = f32[8,1,128]{2,1,0:T(1,128)S(1)} async-done(((f32[8,1,128]{2,1,0:T(1,128)}), f32[8,1,128]{2,1,0:T(1,128)S(1)}, u32[]{:S(2)}, u32[]{:S(2)}) %all-to-all-start.4) | async-done | bytes 4128 | tf_op jit(solution)/shard_map/all_to_all | solution.py:128
  277.2 3.4 %all-to-all-start.3 = ((bf16[4,32,1024]{2,1,0:T(8,128)(2,1)}), bf16[4,32,1024]{2,1,0:T(8,128)(2,1)S(1)}, u32[]{:S(2)}, u32[]{:S(2)}) async-start(bf16[4,32,1024]{2,1,0:T(8,128)(2,1)} %pad_maximum_fusion.14), calls=%async_computation.3 | async-start | bytes 524288 | tf_op jit(solution)/shard_map/all_to_all | solution.py:117
  280.6 2.2 fusion.49
  282.8 1.9 pad_maximum_fusion.1
  286.6 3.1 %all-to-all-done.3 = bf16[4,32,1024]{2,1,0:T(8,128)(2,1)S(1)} async-done(((bf16[4,32,1024]{2,1,0:T(8,128)(2,1)}), bf16[4,32,1024]{2,1,0:T(8,128)(2,1)S(1)}, u32[]{:S(2)}, u32[]{:S(2)}) %all-to-all-start.3) | async-done | bytes 262176 | tf_op jit(solution)/shard_map/all_to_all | solution.py:117
  (136 shorter events, 13.8 us)
Async XLA Ops:
  7.2 16.9 %copy-start.34 = (s32[16,8]{0,1:T(8,128)S(1)}, s32[16,8]{0,1:T(8,128)}, u32[]{:S(2)}) copy-start(s32[16,8]{0,1:T(8,128)} %param.9) | copy-start | bytes 1540
  7.2 16.9 %copy-start.35 = (f32[16,8]{0,1:T(8,128)S(1)}, f32[16,8]{0,1:T(8,128)}, u32[]{:S(2)}) copy-start(f32[16,8]{0,1:T(8,128)} %param.11) | copy-start | bytes 1540
  7.2 58.8 %all-gather.3.cloned.1.call-start = ((), (), s32[]{:S(2)}) async-start(), calls=%async_computation.5 | async-start | bytes 1179648 | tf_op jit(solution)/shard_map/all_gather | solution.py:44
  8.2 57.9 %copy-start.36 = (s32[8]{0:T(128)S(1)}, s32[8]{0:T(128)}, u32[]{:S(2)}) copy-start(s32[8]{0:T(128)} %param.10) | copy-start | bytes 100
  24.0 61.9 %all-gather.5.cloned.1.call-start = ((), (), s32[]{:S(2)}) async-start(), calls=%async_computation.6 | async-start | bytes 1179648 | tf_op jit(solution)/shard_map/all_gather | solution.py:44
  65.4 11.3 %copy-start.32 = (s32[3]{0:T(128)}, s32[3]{0:T(128)S(1)}, u32[]{:S(2)}) copy-start(s32[3]{0:T(128)S(1)} %pad_add_fusion) | copy-start | bytes 40
  66.0 98.8 %all-reduce.6.cloned.1.call-start = ((), (), s32[]{:S(2)}) async-start(), calls=%async_computation.8 | async-start | bytes 3538944 | tf_op jit(solution)/shard_map/psum | solution.py:88
  66.1 10.7 %copy-start.26 = (s32[3,512]{1,0:T(4,128)}, s32[3,512]{1,0:T(4,128)S(1)}, u32[]{:S(2)}) copy-start(s32[3,512]{1,0:T(4,128)S(1)} %add_select_fusion) | copy-start | bytes 18436
  67.7 2.3 copy-start
  70.0 4.5 %copy-start.11 = (bf16[576,1024]{1,0:T(8,128)(2,1)}, bf16[576,1024]{1,0:T(8,128)(2,1)S(1)}, u32[]{:S(2)}) copy-start(bf16[576,1024]{1,0:T(8,128)(2,1)S(1)} %convolution_convert_fusion.6) | copy-start | bytes 3538948
  70.0 3.1 %copy-start.6 = (bf16[2,1024,768]{2,1,0:T(8,128)(2,1)S(1)}, bf16[2,1024,768]{2,1,0:T(8,128)(2,1)}, u32[]{:S(2)}) copy-start(bf16[2,1024,768]{2,1,0:T(8,128)(2,1)} %param.14) | copy-start | bytes 9437188
  76.5 137.0 %all-reduce.4.cloned.1.call-start = ((), (), s32[]{:S(2)}) async-start(), calls=%async_computation.7 | async-start | bytes 1769472 | tf_op jit(solution)/shard_map/psum | solution.py:90
  77.1 11.0 %copy-start.30 = (f32[3,192]{1,0:T(4,128)}, f32[3,192]{1,0:T(4,128)S(1)}, u32[]{:S(2)}) copy-start(f32[3,192]{1,0:T(4,128)S(1)} %select_reduce_fusion.1) | copy-start | bytes 6916
  85.9 2.2 copy-start.4
  88.1 1.4 copy-start.9
  164.9 2.2 copy-start.10
  213.6 4.9 %copy-start.5 = (bf16[2,768,1024]{2,1,0:T(8,128)(2,1)S(1)}, bf16[2,768,1024]{2,1,0:T(8,128)(2,1)}, u32[]{:S(2)}) copy-start(bf16[2,768,1024]{2,1,0:T(8,128)(2,1)} %param.15) | copy-start | bytes 9437188
  216.6 2.3 copy-start.1
  216.6 6.6 %copy-start.2 = (bf16[3,192,768]{2,1,0:T(8,128)(2,1)}, bf16[3,192,768]{2,1,0:T(8,128)(2,1)S(1)}, u32[]{:S(2)}) copy-start(bf16[3,192,768]{2,1,0:T(8,128)(2,1)S(1)} %get-tuple-element.21) | copy-start | bytes 2654212
  219.4 2.2 copy-start.7
  223.2 1.6 copy-start.31
  223.2 1.6 copy-start.27
  223.2 1.8 copy-start.33
  227.8 22.2 %all-to-all-start.1 = ((bf16[8,64,1024]{2,1,0:T(8,128)(2,1)}), bf16[8,64,1024]{2,1,0:T(8,128)(2,1)}, u32[]{:S(2)}, u32[]{:S(2)}) async-start(bf16[8,64,1024]{2,1,0:T(8,128)(2,1)} %bitcast.232), calls=%async_computation.1 | async-start | bytes 2097152 | tf_op jit(solution)/shard_map/all_to_all | solution.py:100
  232.2 2.8 copy-start.8
  235.0 2.5 copy-start.16
  235.0 2.5 copy-start.17
  235.0 2.5 copy-start.21
  235.0 2.5 copy-start.23
  237.5 1.0 copy-start.15
  237.5 1.1 copy-start.22
  239.6 2.0 copy-start.12
  239.6 2.0 copy-start.24
  239.6 2.0 copy-start.25
  241.6 2.2 copy-start.29
  246.1 1.7 copy-start.18
  246.1 1.7 copy-start.19
  246.2 1.7 copy-start.28
  249.9 4.0 %copy-start.20 = (bf16[192,1024]{1,0:T(8,128)(2,1)S(1)}, bf16[192,1024]{1,0:T(8,128)(2,1)}, u32[]{:S(2)}) copy-start(bf16[192,1024]{1,0:T(8,128)(2,1)} %get-tuple-element.26) | copy-start | bytes 1179652
  249.9 19.4 %all-to-all-start.2 = ((bf16[8,64,1024]{2,1,0:T(8,128)(2,1)}), bf16[8,64,1024]{2,1,0:T(8,128)(2,1)S(1)}, u32[]{:S(2)}, u32[]{:S(2)}) async-start(bf16[8,64,1024]{2,1,0:T(8,128)(2,1)} %bitcast.48), calls=%async_computation.2 | async-start | bytes 2097152 | tf_op jit(solution)/shard_map/all_to_all | solution.py:100
  254.0 4.2 %copy-start.14 = (bf16[1,1024,768]{2,1,0:T(8,128)(2,1)S(1)}, bf16[1,1024,768]{2,1,0:T(8,128)(2,1)}, u32[]{:S(2)}) copy-start(bf16[1,1024,768]{2,1,0:T(8,128)(2,1)} %fusion.48) | copy-start | bytes 4718596
  258.1 3.4 %copy-start.3 = (bf16[3,192,768]{2,1,0:T(8,128)(2,1)S(1)}, bf16[3,192,768]{2,1,0:T(8,128)(2,1)}, u32[]{:S(2)}) copy-start(bf16[3,192,768]{2,1,0:T(8,128)(2,1)} %copy-done.2) | copy-start | bytes 2654212
  261.6 1.5 copy-start.13
  269.4 7.8 %all-to-all-start.4 = ((f32[8,1,128]{2,1,0:T(1,128)}), f32[8,1,128]{2,1,0:T(1,128)S(1)}, u32[]{:S(2)}, u32[]{:S(2)}) async-start(f32[8,1,128]{2,1,0:T(1,128)} %reshape.139), calls=%async_computation.4 | async-start | bytes 8192 | tf_op jit(solution)/shard_map/all_to_all | solution.py:128
  277.2 12.5 %all-to-all-start.3 = ((bf16[4,32,1024]{2,1,0:T(8,128)(2,1)}), bf16[4,32,1024]{2,1,0:T(8,128)(2,1)S(1)}, u32[]{:S(2)}, u32[]{:S(2)}) async-start(bf16[4,32,1024]{2,1,0:T(8,128)(2,1)} %pad_maximum_fusion.14), calls=%async_computation.3 | async-start | bytes 524288 | tf_op jit(solution)/shard_map/all_to_all | solution.py:117
Sparse Core Ops, SparseCore 0:
  24.1 22.9 all-gather.2
  66.2 19.6 all-gather.4
  88.9 75.8 all-reduce.5
  167.7 45.7 all-reduce.3

commit v3 on v1

--- a/solution.py
+++ b/solution.py
@@ -30,18 +30,28 @@
     host = (me + half) % owners
     lent = replicas[host] - me * per_owner
 
-    routing = jnp.concatenate([units.astype(F32), route_probs], axis=1)
-    routing = lax.all_gather(routing, ("dp", "expert"), axis=0, tiled=True)
-    routing = routing.reshape(groups, owners, tok, 2 * top).transpose(1, 0, 2, 3)
-    routing = routing.reshape(total, 2 * top)
-    all_units = routing[:, :top].astype(jnp.int32)
-    all_probs = routing[:, top:]
-    both = jnp.concatenate([tokens, cotangent], axis=0)
-    both = lax.all_to_all(both, "dp", split_axis=1, concat_axis=0, tiled=True)
+    high = lax.reduce_precision(route_probs, 8, 7)
+    middle = lax.reduce_precision(route_probs - high, 8, 7)
+    low = route_probs - high - middle
+    routing = jnp.concatenate([units.astype(F32), high, middle, low], axis=1).astype(BF)
+    side = 128 * ((4 * top + 127) // 128)
+    routing = jnp.pad(routing, ((0, 0), (0, side - 4 * top)))
+    rows = jnp.concatenate([tokens, cotangent], axis=0)
+    routing = jnp.concatenate([routing, jnp.zeros_like(routing)], axis=0)
+    pieces = []
+    for g in range(groups):
+        pieces.append(
+            jnp.concatenate([rows[:, g * width : (g + 1) * width], routing], axis=1)
+        )
+    both = jnp.concatenate(pieces, axis=0)
+    both = lax.all_to_all(both, "dp", split_axis=0, concat_axis=0, tiled=True)
     both = lax.all_gather(both, "expert", axis=0, tiled=True)
-    both = both.reshape(blocks, 2, tok, width)
-    all_tokens = both[:, 0].reshape(total, width)
-    all_cot = both[:, 1].reshape(total, width)
+    both = both.reshape(blocks, 2, tok, width + side)
+    all_tokens = both[:, 0, :, :width].reshape(total, width)
+    all_cot = both[:, 1, :, :width].reshape(total, width)
+    routing = both[:, 0, :, width : width + 4 * top].reshape(total, 4, top).astype(F32)
+    all_units = routing[:, 0].astype(jnp.int32)
+    all_probs = routing[:, 1] + routing[:, 2] + routing[:, 3]
 
     mine = jnp.concatenate(
         [
@@ -96,14 +106,28 @@
     grad_gate = (grad_hidden * up * sig * (1.0 + gate * (1.0 - sig))).astype(BF)
     grad_up = (grad_hidden * silu).astype(BF)
 
-    def send_back(rows):
-        part = dot("st,sd->td", flat_select, rows.reshape(per_unit * slots, width)).astype(BF)
+    filled = slot_probs > 0.0
+    dots = jnp.sum(hidden.astype(F32) * grad_hidden, axis=2) / jnp.where(filled, slot_probs, 1.0)
+    per_token = jnp.sum(jnp.where(chosen, dots[:, :, None], 0.0), axis=1)
+    spread = jnp.sum(jnp.where(match, per_token[:, :, None], 0.0), axis=0)
+    spread_high = lax.reduce_precision(spread, 8, 7)
+    spread = jnp.concatenate([spread_high, spread - spread_high], axis=1).astype(BF)
+    spread = jnp.pad(spread, ((0, 0), (0, side - 2 * top)))
+
+    def combined(rows):
+        return dot("st,sd->td", flat_select, rows.reshape(per_unit * slots, width)).astype(BF)
+
+    def send_back(part):
         part = lax.all_to_all(part, "expert", split_axis=0, concat_axis=0, tiled=True)
-        part = part.reshape(owners, groups, tok, width)
-        return jnp.sum(part.astype(F32), axis=0).astype(BF)
+        part = part.reshape(owners, groups, tok, -1)
+        return jnp.sum(part.astype(F32), axis=0)
 
     expert_out = jnp.stack([dot("sf,fd->sd", hidden[u], at(w_down, u)) for u in range(per_unit)])
-    out_part = send_back((slot_probs[:, :, None] * expert_out).astype(BF))
+    out_part = combined((slot_probs[:, :, None] * expert_out).astype(BF))
+    out_part = send_back(jnp.concatenate([out_part, spread], axis=1))
+    d_probs = lax.dynamic_index_in_dim(out_part[:, :, width:], my_group, 0, keepdims=False)
+    d_probs = d_probs[:, :top] + d_probs[:, top : 2 * top]
+    out_part = out_part[:, :, :width].astype(BF)
     expert_grad = jnp.stack(
         [
             (
@@ -113,30 +137,18 @@
             for u in range(per_unit)
         ]
     )
-    grad_part = send_back(expert_grad)
+    grad_part = send_back(combined(expert_grad)).astype(BF)
     last = jnp.concatenate([out_part, grad_part], axis=1).reshape(groups * 2 * tok, width)
     last = lax.all_to_all(last, "dp", split_axis=0, concat_axis=1, tiled=True)
     layer_out = last[:tok]
     d_tokens = last[tok:]
 
-    filled = slot_probs > 0.0
-    dots = jnp.sum(hidden.astype(F32) * grad_hidden, axis=2) / jnp.where(filled, slot_probs, 1.0)
-    per_token = jnp.sum(jnp.where(chosen, dots[:, :, None], 0.0), axis=1)
-    spread = jnp.sum(jnp.where(match, per_token[:, :, None], 0.0), axis=0)
-    spread = lax.dynamic_index_in_dim(
-        spread.reshape(owners, groups, tok, top), my_group, 1, keepdims=False
-    )
-    spread = lax.all_to_all(spread, "expert", split_axis=0, concat_axis=0, tiled=True)
-    d_probs = jnp.sum(spread, axis=0)
-
     def weight_grads(left, right):
-        grads = []
-        for e in range(per_owner):
-            marked = jnp.where(lent == e, 1.0, 0.0).astype(BF)
-            a = jnp.concatenate([left[e], left[per_owner]], axis=0)
-            b = jnp.concatenate([right[e], right[per_owner] * marked], axis=0)
-            grads.append(dot("sa,sb->ab", a, b).astype(BF))
-        return jnp.stack(grads)
+        marked = (jnp.arange(per_owner, dtype=jnp.int32) == lent).astype(BF)[:, None, None]
+        extra = jnp.broadcast_to(left[per_owner:], left[:per_owner].shape)
+        a = jnp.concatenate([left[:per_owner], extra], axis=1)
+        b = jnp.concatenate([right[:per_owner], right[per_owner:] * marked], axis=1)
+        return dot("esa,esb->eab", a, b).astype(BF)
 
     d_gate_w = weight_grads(xs, grad_gate)
     d_up_w = weight_grads(xs, grad_up)

time: 268 us -> 254 us (0.948)
  blocking collectives: 55.5 us -> 15.8 us
  waiting for transfers between devices: 110 us -> 144 us
  local copies, waits for them, and re-layouts: 15 us -> 21.4 us
  matrix products: 35 us -> 28.8 us
  other arithmetic: 21.8 us -> 16.1 us
  starting transfers between devices: 15.3 us -> 12.1 us
    all_gather x1 -> x0, blocking collectives: 40.4 us -> none  [local(): routing = lax.all_gather(routing, ('dp', 'expert'), axis=0, tiled=True)]
    all_gather x1, waiting for transfers between devices: 0.02 us -> 26.7 us  [local(): both = lax.all_gather(both, 'expert', axis=0, tiled=True)]
    all_to_all x2, waiting for transfers between devices: 3.84 us -> 17 us  [send_back(): lax.all_to_all(part, 'expert', split_axis=0, concat_axis=0, tiled=True)]
    dot_general x28 -> x25, matrix products: 35 us -> 28.8 us  [dot(): return jnp.einsum(spec, a, b, preferred_element_type=F32)]
    another operation x3, other arithmetic: 7.31 us -> 1.39 us  [weight_grads(): return jnp.stack(grads)]
    slice x1 -> x11, local copies, waits for them, and re-layouts: 1.72 us -> 7.35 us  [the longest x3 4.45 us: weight_grads(): a = jnp.concatenate([left[:per_owner], extra], axis=1)]
    all_to_all x1 -> x0, waiting for transfers between devices: 3.61 us -> none  [local(): lax.all_to_all(spread, 'expert', split_axis=0, concat_axis=0, tiled=True)]
    all_to_all x1 -> x0, starting transfers between devices: 3.31 us -> none  [local(): lax.all_to_all(spread, 'expert', split_axis=0, concat_axis=0, tiled=True)]
  transfers between devices with their start and end apart: 6 -> 5, of which waited for: 4 -> 5; matrix products, arithmetic and copies ran while one was open for 16% -> 10% of each run, Pallas kernels for 0% -> 0%
where the time goes in v3:
time: 254 us; the launch traced here: 253 us
  waiting for transfers between devices  144 us (57%)
  matrix products  28.8 us (11%)
  local copies, waits for them, and re-layouts  21.4 us (8%)
  other arithmetic  16.1 us (6%)
  blocking collectives  15.8 us (6%)
  between operations  15.4 us (6%)
  starting transfers between devices  12.1 us (5%)
    psum x1, waiting for transfers between devices, local(): lax.psum((per('sd,df->sf', xs, w_gate), per('sd,df->sf', xs, w_up), per('...  97.5 us
    dot_general x25, matrix products, dot(): return jnp.einsum(spec, a, b, preferred_element_type=F32)  28.8 us
    all_gather x1, waiting for transfers between devices, local(): both = lax.all_gather(both, 'expert', axis=0, tiled=True)  26.7 us
    all_to_all x2, waiting for transfers between devices, send_back(): lax.all_to_all(part, 'expert', split_axis=0, concat_axis=0, tiled=True)  17 us
    all_to_all x1, blocking collectives, local(): both = lax.all_to_all(both, 'dp', split_axis=0, concat_axis=0, tiled=True)  15.8 us
    all_to_all x2, starting transfers between devices, send_back(): lax.all_to_all(part, 'expert', split_axis=0, concat_axis=0, tiled=True)  8.63 us
    unnamed x58, local copies, waits for them, and re-layouts  7.62 us
  transfers between devices with their start and end apart: 5, of which 5 were waited for; matrix products, arithmetic and copies ran while one was open for 10% of the time, Pallas kernels for 0%

profile of v3, /device:TPU:0, one launch (start us, length us, event | category | flops | bytes accessed | tf_op | source)
XLA Modules:
  0.0 253.3 jit_solution(16367229107897007076)
XLA Ops:
  7.2 0.7 reduce-precision_convert_fusion.2
  7.9 0.7 convert_convert_fusion
  8.7 0.9 constant_dynamic-update-slice_fusion.1
  9.6 0.9 constant_dynamic-update-slice_fusion
  10.6 15.8 %all_to_all.43 = bf16[4,32,1152]{2,1,0:T(8,128)(2,1)} all-to-all(bf16[4,32,1152]{2,1,0:T(8,128)(2,1)S(1)} %bitcast.207), channel_id=1, replica_groups=mesh['dp'=4,'expert'=8] {'dp'}, dimensions={0} | all-to-all | bytes 589824 | tf_op jit(solution)/shard_map/all_to_all | solution.py:47
  28.0 26.7 %all-gather.2.cloned.1.call-done = bf16[1024,1152]{1,0:T(8,128)(2,1)} async-done(((bf16[128,1152]{1,0:T(8,128)(2,1)}), bf16[1024,1152]{1,0:T(8,128)(2,1)}) %all-gather.2.cloned.1.call-update) | async-done | bytes 2359312 | tf_op jit(solution)/shard_map/all_gather | solution.py:48
  54.7 0.9 slice_convert_fusion.1
  55.7 2.8 %fusion.207 = (bf16[32,1,16,1024]{3,2,1,0:T(8,128)(2,1)}, bf16[32,1,16,1024]{3,2,1,0:T(8,128)(2,1)S(1)}) fusion(bf16[32,2,16,1152]{3,2,1,0:T(8,128)(2,1)} %bitcast.204), kind=kLoop, calls=%fused_computation.214 | loop fusion | bytes 4194304 | tf_op jit(solution)/shard_map/slice | solution.py:50
  60.4 0.8 multiply_convert_fusion
  61.2 1.1 copy-done.10
  62.3 0.7 fusion.158
  62.9 0.7 fusion.161
  63.7 0.7 fusion.149
  64.9 0.8 convolution_convert_fusion.3
  65.7 1.1 copy-done
  68.2 0.9 copy-done.8
  70.6 1.0 pad_maximum_fusion.5
  71.6 1.4 pad_maximum_fusion.3
  73.6 2.1 slice.243
  75.7 1.0 slice-done
  76.7 1.0 copy.78
  77.7 2.3 copy.79
  80.0 1.6 broadcast_multiply_fusion
  81.6 97.5 %all-reduce.6.cloned.1.call-done = (bf16[3,192,768]{2,1,0:T(8,128)(2,1)}, bf16[3,192,768]{2,1,0:T(8,128)(2,1)}, bf16[3,192,768]{2,1,0:T(8,128)(2,1)}) async-done(((bf16[3,192,768]{2,1,0:T(8,128)(2,1)}, bf16[3,192,768]{2,1,0:T(8,128)(2,1)}, bf16[3,192,768]{2,1,0:T(8,128)(2,1)}), (bf16[3,192,768]{2,1,0:T(8,128)(2,1)}, bf16[3,192,768]{2,1,0:T(8,128)(2,1)}, ...) | async-done | bytes 2654224 | tf_op jit(solution)/shard_map/psum | solution.py:94
  179.1 3.0 %fusion.9 = (f32[3,192]{1,0:T(4,128)S(1)}, bf16[3,192,768]{2,1,0:T(8,128)(2,1)S(1)}, bf16[3,192,768]{2,1,0:T(8,128)(2,1)S(1)}, bf16[3,192,768]{2,1,0:T(8,128)(2,1)S(1)}) fusion(bf16[3,192,768]{2,1,0:T(8,128)(2,1)} %get-tuple-element.30, bf16[3,192,768]{2,1,0:T(8,128)(2,1)} %get-tuple-element.32, bf16[3,192,768]{2,1,0:T(8,128)(2,1)} %get-tuple-element.31), kind=kLoop, calls=%fused_computation.25 | loop fusion | flops 9289152 | bytes 5310720 | tf_op jit(solution)/shard_map/reduce_sum | solution.py:110
  184.2 0.8 copy-done.11
  185.0 1.4 fusion.81
  186.4 1.4 fusion.78
  188.4 0.7 fusion.126
  189.1 0.7 fusion.123
  189.8 2.0 bitcast_convert_fusion
  191.8 4.4 %all-to-all-start.2 = ((bf16[8,64,1024]{2,1,0:T(8,128)(2,1)}), bf16[8,64,1024]{2,1,0:T(8,128)(2,1)}, u32[]{:S(2)}, u32[]{:S(2)}) async-start(bf16[8,64,1024]{2,1,0:T(8,128)(2,1)} %bitcast.47), calls=%async_computation.2 | async-start | bytes 2097152 | tf_op jit(solution)/shard_map/all_to_all | solution.py:121
  196.7 2.0 fusion.84
  198.8 1.1 bitcast_convert_fusion.1
  199.9 1.1 fusion.132
  201.0 10.6 %all-to-all-done.2 = bf16[8,64,1024]{2,1,0:T(8,128)(2,1)} async-done(((bf16[8,64,1024]{2,1,0:T(8,128)(2,1)}), bf16[8,64,1024]{2,1,0:T(8,128)(2,1)}, u32[]{:S(2)}, u32[]{:S(2)}) %all-to-all-start.2) | async-done | bytes 1048608 | tf_op jit(solution)/shard_map/all_to_all | solution.py:121
  211.6 4.3 %all-to-all-start.1 = ((bf16[8,64,1152]{2,1,0:T(8,128)(2,1)}), bf16[8,64,1152]{2,1,0:T(8,128)(2,1)}, u32[]{:S(2)}, u32[]{:S(2)}) async-start(bf16[8,64,1152]{2,1,0:T(8,128)(2,1)} %bitcast.201), calls=%async_computation.1 | async-start | bytes 2359296 | tf_op jit(solution)/shard_map/all_to_all | solution.py:121
  217.8 3.5 %convolution_convert_fusion.2 = bf16[2,1024,768]{2,1,0:T(8,128)(2,1)} fusion(bf16[2,192,1024]{1,2,0:T(8,128)(2,1)S(1)} %broadcast_in_dim.95, bf16[2,192,1024]{1,2,0:T(8,128)(2,1)S(1)} %copy-done.14, bf16[2,192,768]{2,1,0:T(8,128)(2,1)S(1)} %get-tuple-element.53, bf16[2,192,768]{2,1,0:T(8,128)(2,1)S(1)} %slice.244), kind=kOutput, calls=%fused_computation.14 | convolution fusion | flops 1215037440 | bytes 5898240 | tf_op jit(solution)/shard_map/esa,esb->eab/dot_general | solution.py:11
  221.3 3.5 %convolution_convert_fusion.1 = bf16[2,1024,768]{2,1,0:T(8,128)(2,1)} fusion(bf16[2,192,1024]{1,2,0:T(8,128)(2,1)S(1)} %broadcast_in_dim.95, bf16[2,192,1024]{1,2,0:T(8,128)(2,1)S(1)} %copy-done.14, bf16[2,192,768]{2,1,0:T(8,128)(2,1)S(1)} %get-tuple-element.52, bf16[2,192,768]{2,1,0:T(8,128)(2,1)S(1)} %slice.245), kind=kOutput, calls=%fused_computation.13 | convolution fusion | flops 1215037440 | bytes 5898240 | tf_op jit(solution)/shard_map/esa,esb->eab/dot_general | solution.py:11
  224.8 1.4 reduce_sum.90
  226.3 6.4 %all-to-all-done.1 = bf16[8,64,1152]{2,1,0:T(8,128)(2,1)} async-done(((bf16[8,64,1152]{2,1,0:T(8,128)(2,1)}), bf16[8,64,1152]{2,1,0:T(8,128)(2,1)}, u32[]{:S(2)}, u32[]{:S(2)}) %all-to-all-start.1) | async-done | bytes 1179680 | tf_op jit(solution)/shard_map/all_to_all | solution.py:121
  232.7 1.5 convert_reduce_fusion
  234.2 0.7 pad_maximum_fusion.6
  234.9 3.4 %all-to-all-start.3 = ((bf16[4,32,1024]{2,1,0:T(8,128)(2,1)}), bf16[4,32,1024]{2,1,0:T(8,128)(2,1)S(1)}, u32[]{:S(2)}, u32[]{:S(2)}) async-start(bf16[4,32,1024]{2,1,0:T(8,128)(2,1)} %pad_maximum_fusion.6), calls=%async_computation.3 | async-start | bytes 524288 | tf_op jit(solution)/shard_map/all_to_all | solution.py:142
  238.4 3.5 %convolution_convert_fusion = bf16[2,768,1024]{2,1,0:T(8,128)(2,1)} fusion(bf16[2,192,1024]{2,1,0:T(8,128)(2,1)S(1)} %copy-done.16, bf16[2,192,1024]{2,1,0:T(8,128)(2,1)S(1)} %bitcast.205, bf16[2,192,768]{2,1,0:T(8,128)(2,1)S(1)} %broadcast_in_dim.96, bf16[2,192,768]{2,1,0:T(8,128)(2,1)S(1)} %slice.246), kind=kOutput, calls=%fused_computation.12 | convolution fusion | flops 1215037440 | bytes 5898240 | tf_op jit(solution)/shard_map/esa,esb->eab/dot_general | solution.py:11
  242.0 0.7 copy.81
  242.7 2.4 all-to-all-done.3
  245.1 0.7 copy.85
  (118 shorter events, 12.8 us)
Async XLA Ops:
  7.2 19.3 %copy-start.24 = (s32[8]{0:T(128)S(1)}, s32[8]{0:T(128)}, u32[]{:S(2)}) copy-start(s32[8]{0:T(128)} %param.10) | copy-start | bytes 100
  7.2 47.5 %all-gather.2.cloned.1.call-start = ((), (), s32[]{:S(2)}) async-start(), calls=%async_computation.4 | async-start | bytes 2654208 | tf_op jit(solution)/shard_map/all_gather | solution.py:48
  26.4 152.7 %all-reduce.6.cloned.1.call-start = ((), (), s32[]{:S(2)}) async-start(), calls=%async_computation.5 | async-start | bytes 5308416 | tf_op jit(solution)/shard_map/psum | solution.py:94
  28.0 32.0 %copy-start.21 = (s32[3]{0:T(128)}, s32[3]{0:T(128)S(1)}, u32[]{:S(2)}) copy-start(s32[3]{0:T(128)S(1)} %pad_add_fusion) | copy-start | bytes 40
  59.8 1.4 copy-start.17
  60.3 0.9 copy-start.19
  60.4 1.9 copy-start.10
  62.3 1.4 copy-start.13
  63.6 1.2 copy-start.15
  64.9 1.9 copy-start
  66.8 3.4 %copy-start.7 = (bf16[576,1024]{1,0:T(8,128)(2,1)}, bf16[576,1024]{1,0:T(8,128)(2,1)S(1)}, u32[]{:S(2)}) copy-start(bf16[576,1024]{1,0:T(8,128)(2,1)S(1)} %convolution_convert_fusion.3) | copy-start | bytes 3538948
  67.2 1.9 copy-start.8
  75.7 1.0 slice-start
  77.7 2.3 slice-start.1
  179.1 3.1 %copy-start.9 = (bf16[2,1024,768]{2,1,0:T(8,128)(2,1)S(1)}, bf16[2,1024,768]{2,1,0:T(8,128)(2,1)}, u32[]{:S(2)}) copy-start(bf16[2,1024,768]{2,1,0:T(8,128)(2,1)} %param.14) | copy-start | bytes 9437188
  182.2 1.4 copy-start.5
  182.2 4.2 %copy-start.3 = (bf16[3,192,768]{2,1,0:T(8,128)(2,1)}, bf16[3,192,768]{2,1,0:T(8,128)(2,1)S(1)}, u32[]{:S(2)}) copy-start(bf16[3,192,768]{2,1,0:T(8,128)(2,1)S(1)} %get-tuple-element.34) | copy-start | bytes 2654212
  182.2 6.9 %copy-start.1 = (bf16[3,192,768]{2,1,0:T(8,128)(2,1)}, bf16[3,192,768]{2,1,0:T(8,128)(2,1)S(1)}, u32[]{:S(2)}) copy-start(bf16[3,192,768]{2,1,0:T(8,128)(2,1)S(1)} %get-tuple-element.35) | copy-start | bytes 2654212
  182.9 2.1 copy-start.11
  189.1 0.7 copy-start.18
  191.8 4.4 %copy-start.20 = (f32[3,192]{1,0:T(4,128)S(1)}, f32[3,192]{1,0:T(4,128)}, u32[]{:S(2)}) copy-start(f32[3,192]{1,0:T(4,128)} %copy-done.19) | copy-start | bytes 6916
  191.8 4.7 %copy-start.22 = (s32[3]{0:T(128)S(1)}, s32[3]{0:T(128)}, u32[]{:S(2)}) copy-start(s32[3]{0:T(128)} %copy-done.21) | copy-start | bytes 40
  191.8 4.9 %copy-start.4 = (bf16[3,192,768]{2,1,0:T(8,128)(2,1)S(1)}, bf16[3,192,768]{2,1,0:T(8,128)(2,1)}, u32[]{:S(2)}) copy-start(bf16[3,192,768]{2,1,0:T(8,128)(2,1)} %copy-done.3) | copy-start | bytes 2654212
  191.8 19.8 %all-to-all-start.2 = ((bf16[8,64,1024]{2,1,0:T(8,128)(2,1)}), bf16[8,64,1024]{2,1,0:T(8,128)(2,1)}, u32[]{:S(2)}, u32[]{:S(2)}) async-start(bf16[8,64,1024]{2,1,0:T(8,128)(2,1)} %bitcast.47), calls=%async_computation.2 | async-start | bytes 2097152 | tf_op jit(solution)/shard_map/all_to_all | solution.py:121
  196.2 2.6 %copy-start.6 = (bf16[3,192,768]{2,1,0:T(8,128)(2,1)S(1)}, bf16[3,192,768]{2,1,0:T(8,128)(2,1)}, u32[]{:S(2)}) copy-start(bf16[3,192,768]{2,1,0:T(8,128)(2,1)} %copy-done.5) | copy-start | bytes 2654212
  196.7 2.1 copy-start.25
  196.7 2.1 copy-start.26
  201.0 14.9 %copy-start.2 = (bf16[3,192,768]{2,1,0:T(8,128)(2,1)S(1)}, bf16[3,192,768]{2,1,0:T(8,128)(2,1)}, u32[]{:S(2)}) copy-start(bf16[3,192,768]{2,1,0:T(8,128)(2,1)} %copy-done.1) | copy-start | bytes 2654212
  211.6 21.1 %all-to-all-start.1 = ((bf16[8,64,1152]{2,1,0:T(8,128)(2,1)}), bf16[8,64,1152]{2,1,0:T(8,128)(2,1)}, u32[]{:S(2)}, u32[]{:S(2)}) async-start(bf16[8,64,1152]{2,1,0:T(8,128)(2,1)} %bitcast.201), calls=%async_computation.1 | async-start | bytes 2359296 | tf_op jit(solution)/shard_map/all_to_all | solution.py:121
  215.9 0.6 copy-start.23
  216.0 1.0 copy-start.12
  216.5 1.3 copy-start.14
  226.2 12.1 %slice-start.2 = ((bf16[576,1024]{1,0:T(8,128)(2,1)}), bf16[384,1024]{1,0:T(8,128)(2,1)S(1)}, s32[]{:S(2)}) async-start(bf16[576,1024]{1,0:T(8,128)(2,1)} %copy-done.13), calls=%async_computation.8 | async-start | bytes 1572864 | tf_op jit(solution)/shard_map/slice | solution.py:150
  226.3 12.1 %copy-start.16 = (bf16[2,192,1024]{2,1,0:T(8,128)(2,1)S(1)}, bf16[2,192,1024]{2,1,0:T(8,128)(2,1)}, u32[]{:S(2)}) copy-start(bf16[2,192,1024]{2,1,0:T(8,128)(2,1)} %broadcast_multiply_fusion) | copy-start | bytes 2359300
  234.9 10.2 %all-to-all-start.3 = ((bf16[4,32,1024]{2,1,0:T(8,128)(2,1)}), bf16[4,32,1024]{2,1,0:T(8,128)(2,1)S(1)}, u32[]{:S(2)}, u32[]{:S(2)}) async-start(bf16[4,32,1024]{2,1,0:T(8,128)(2,1)} %pad_maximum_fusion.6), calls=%async_computation.3 | async-start | bytes 524288 | tf_op jit(solution)/shard_map/all_to_all | solution.py:142
Sparse Core Ops, SparseCore 0:
  26.6 28.1 all-gather.1
  73.2 105.8 all-reduce.5
